TPU v7x, 256 devices: a whole 4x4x8 slice. The times are simulated.
256 devices in a mesh: dp: 4 (over x), head: 4 (over y), ctx: 16 (over z, core).
Axes of the slice: x: 4, y: 4, z: 8, core: 2. Of those that a mesh axis runs over, the one named last changes fastest.
Arguments:
- q_count: int32 [4, 8192, 3584], P('dp', 'ctx', 'head'), may hold values from 0 to 4
- k_count: int32 [4, 8192, 3584], P('dp', 'ctx', 'head'), may hold values from 0 to 4
- v_count: int32 [4, 8192, 3584], P('dp', 'ctx', 'head'), may hold values from 0 to 4
- q_pre: bfloat16 [4, 8192, 3584], P('dp', 'ctx', 'head'), may hold values from -6 to 6
- k_pre: bfloat16 [4, 8192, 3584], P('dp', 'ctx', 'head'), may hold values from -6 to 6
- v_pre: bfloat16 [4, 8192, 3584], P('dp', 'ctx', 'head'), may hold values from -6 to 6
- grad_y: bfloat16 [4, 8192, 3584], P('dp', 'ctx', 'head'), may hold values from -6 to 6
- gain: float32 [3584], P('head'), may hold values from 0.25 to 1.75
Outputs:
- grad_q_pre: bfloat16 [4, 8192, 3584], P('dp', 'ctx', 'head')
- grad_k_pre: bfloat16 [4, 8192, 3584], P('dp', 'ctx', 'head')
- grad_v_pre: bfloat16 [4, 8192, 3584], P('dp', 'ctx', 'head')
- grad_gain: float32 [3584], P('head')
Inputs may be any that keep to these rules, and one draw needn't show every extreme that they name: `q_count`: each count is how many of the 4 steps fired. `k_count`: each count is how many of the 4 steps fired. `v_count`: each count is how many of the 4 steps fired.
All inputs are finite; a program needn't handle non-finite values.
Results may differ from a plain program's by a relative error of at most 0.001.
Values sent between devices are 32-bit elements; how exact they have to be, the bound alone decides.
No kernel may reach another device: no remote copies, remote signals or barrier semaphores. Data moves between devices by JAX's collectives and lax.ppermute only.
A program may use at most 128 MiB of HBM per device.

v0:
```python
import math

import jax
import jax.numpy as jnp
from jax import lax
from jax.sharding import PartitionSpec as P

E = 128
SPIKE_STEPS = 4


HIGHEST = lax.Precision.HIGHEST


def entering(value, axis, join, neutral, backward):
    count, mine = (lax.axis_size(axis), lax.axis_index(axis))
    pieces = lax.all_gather(value, axis)
    if backward:
        pieces = pieces[::-1]
        mine = count - 1 - mine
    running = jnp.full_like(value, 0) + jnp.asarray(neutral, value.dtype)

    def lap(position, running):
        longer = join(running, pieces[position])
        return jnp.where(position < mine, longer, running)

    return lax.fori_loop(0, count - 1, lap, running)


def spike_values(count):
    return (count.astype(jnp.float32) - SPIKE_STEPS / 2) * 0.5


def surrogate(pre):
    value = pre.astype(jnp.float32)
    total = jnp.zeros_like(value)
    for level in range(SPIKE_STEPS):
        switch = jax.nn.sigmoid(4.0 * (value - level + (SPIKE_STEPS - 1) / 2))
        total = total + 2.0 * switch * (1.0 - switch)
    return total


def add_one(first, second):
    return first + second


def per_device(q_count, k_count, v_count, q_pre, k_pre, v_pre, grad_y, gain):
    rows = q_count.shape[1]
    width = q_count.shape[2]
    heads_here = width // E
    block = min(512, rows)
    blocks = rows // block
    length = rows * lax.axis_size("ctx")
    factor = 1.0 / math.sqrt(E * length)

    def split(array):
        return array[0].reshape(blocks, block, heads_here, E)

    q_spike = split(spike_values(q_count))
    k_spike = split(spike_values(k_count))
    v_spike = split(spike_values(v_count))
    q_short = q_spike.astype(jnp.bfloat16)
    k_short = k_spike.astype(jnp.bfloat16)
    v_short = v_spike.astype(jnp.bfloat16)
    grad_in = split(grad_y.astype(jnp.float32))
    grad_out = grad_in * gain.reshape(heads_here, E)
    kv_blocks = jnp.einsum("nrhe,nrhf->nhef", k_short, v_short, preferred_element_type=jnp.float32)
    qd_blocks = factor * jnp.einsum("nrhe,nrhf->nhef", q_spike, grad_out, precision=HIGHEST)
    kv_local = jnp.sum(kv_blocks, 0)
    qd_local = jnp.sum(qd_blocks, 0)
    kv_before = jnp.cumsum(kv_blocks, 0) - kv_blocks
    qd_after = qd_local[None] - jnp.cumsum(qd_blocks, 0)
    causal = (
        lax.broadcasted_iota(jnp.int32, (block, block), 0)
        >= lax.broadcasted_iota(jnp.int32, (block, block), 1)
    ).astype(jnp.float32)
    scores = (
        jnp.einsum("nrhe,nshe->nhrs", q_short, k_short, preferred_element_type=jnp.float32) * causal
    )
    weights = jnp.einsum("nrhf,nshf->nhrs", grad_out, v_spike, precision=HIGHEST) * causal
    out_inner = jnp.einsum("nhrs,nshf->nrhf", scores, v_spike, precision=HIGHEST)
    dq_inner = jnp.einsum("nhrs,nshe->nrhe", weights, k_spike, precision=HIGHEST)
    dk_inner = jnp.einsum("nhrs,nrhe->nshe", weights, q_spike, precision=HIGHEST)
    dv_inner = jnp.einsum("nhrs,nrhf->nshf", scores, grad_out, precision=HIGHEST)
    zeros = jnp.zeros_like(kv_local)
    state_in = entering(kv_local, "ctx", add_one, zeros, False)
    grad_after = entering(qd_local, "ctx", add_one, zeros, True)
    state_prev = state_in[None] + kv_before
    grad_next = grad_after[None] + qd_after
    out = factor * (
        out_inner + jnp.einsum("nrhe,nhef->nrhf", q_spike, state_prev, precision=HIGHEST)
    )
    dq_spike = factor * (
        dq_inner + jnp.einsum("nrhf,nhef->nrhe", grad_out, state_prev, precision=HIGHEST)
    )
    dk_spike = factor * dk_inner + jnp.einsum(
        "nrhf,nhef->nrhe", v_spike, grad_next, precision=HIGHEST
    )
    dv_spike = factor * dv_inner + jnp.einsum(
        "nrhe,nhef->nrhf", k_spike, grad_next, precision=HIGHEST
    )
    gain_local = jnp.sum(out * grad_in, axis=(0, 1)).reshape(width)
    grad_gain = lax.psum(gain_local, ("dp", "ctx"))

    def finish(spike_grad, pre):
        return (spike_grad.reshape(1, rows, width) * surrogate(pre)).astype(jnp.bfloat16)

    return (finish(dq_spike, q_pre), finish(dk_spike, k_pre), finish(dv_spike, v_pre), grad_gain)


def solution(mesh):
    placed = (
        P("dp", "ctx", "head"),
        P("dp", "ctx", "head"),
        P("dp", "ctx", "head"),
        P("dp", "ctx", "head"),
        P("dp", "ctx", "head"),
        P("dp", "ctx", "head"),
        P("dp", "ctx", "head"),
        P("head"),
    )
    return jax.shard_map(
        per_device,
        mesh=mesh,
        in_specs=placed,
        out_specs=(
            P("dp", "ctx", "head"),
            P("dp", "ctx", "head"),
            P("dp", "ctx", "head"),
            P("head"),
        ),
        check_vma=False,
    )
```

profile of v0, /device:TPU:16, one launch (start us, length us, event | category | flops | bytes accessed | tf_op | source)
XLA Modules:
  0.0 348.5 jit_solution(13684255308522954894)
XLA Ops:
  7.2 1.5 copy.57
  8.9 2.8 copy.64
  11.8 1.7 add_multiply_fusion
  13.5 1.2 copy-done.3
  14.8 2.8 fusion.91
  17.9 2.7 copy.56
  20.6 2.8 copy.58
  23.4 1.9 add_multiply_fusion.3
  27.3 1.2 fusion.97
  28.5 1.3 copy.63
  29.8 2.3 copy.67
  32.1 1.3 copy.72
  33.5 6.3 %fusion.95 = f32[7,512,512]{2,1,0:T(8,128)} fusion(f32[512,7,128]{0,2,1:T(8,128)} %bitcast.67, f32[512,7,128]{0,2,1:T(8,128)} %bitcast.71), kind=kOutput, calls=%fused_computation.110 | convolution fusion | flops 470679552 | bytes 11010048 | tf_op jit(solution)/shard_map/nrhe,nshe->nhrs/dot_general | solution.py:78
  39.8 8.4 %fusion.89 = f32[7,512,512]{2,1,0:T(8,128)} fusion(f32[512,7,128]{0,2,1:T(8,128)S(1)} %bitcast.64, f32[512,7,128]{0,2,1:T(8,128)S(1)} %bitcast.58, f32[7,128]{1,0:T(8,128)S(1)} %bitcast.77), kind=kOutput, calls=%fused_computation.105 | convolution fusion | flops 2819031040 | bytes 11013632 | tf_op jit(solution)/shard_map/nrhf,nshf->nhrs/dot_general | solution.py:80
  48.2 23.2 %all-gather.7.cloned.1.call-done = f32[112,128,128]{2,1,0:T(8,128)} async-done(((f32[7,128,128]{2,1,0:T(8,128)}), f32[112,128,128]{2,1,0:T(8,128)}) %all-gather.7.cloned.1.call-update) | async-done | bytes 7340048 | tf_op jit(solution)/shard_map/all_gather | solution.py:17
  71.5 7.0 %rev.3 = f32[16,7,128,128]{3,2,1,0:T(8,128)} reverse(f32[16,7,128,128]{3,2,1,0:T(8,128)} %bitcast.74), dimensions={0} | reverse | bytes 14680064 | tf_op jit(solution)/shard_map/rev | solution.py:19
  78.4 18.0 %while.29 = (s32[]{:T(128)}, f32[7,128,128]{2,1,0:T(8,128)S(1)}, s32[]{:T(128)}, f32[16,7,128,128]{3,2,1,0:T(8,128)}, s32[]{:T(128)}, /*index=5*/s32[]{:T(128)}) while((s32[]{:T(128)}, f32[7,128,128]{2,1,0:T(8,128)S(1)}, s32[]{:T(128)}, f32[16,7,128,128]{3,2,1,0:T(8,128)}, s32[]{:T(128)}, /*index=5*/s32[]{:T(128)}) %tuple.68), condition=%wide.region_3.4_spmd.clone, body=%wide.region_2.0_spmd.clone.sunk | while | flops 344068 | bytes 1376357 | solution.py:27
  78.4 1.2 add_select_fusion.5
  79.6 1.2 add_select_fusion.5
  80.8 1.2 add_select_fusion.5
  82.0 1.2 add_select_fusion.5
  83.2 1.2 add_select_fusion.5
  84.4 1.2 add_select_fusion.5
  85.6 1.2 add_select_fusion.5
  86.8 1.2 add_select_fusion.5
  88.0 1.2 add_select_fusion.5
  89.2 1.2 add_select_fusion.5
  90.4 1.2 add_select_fusion.5
  91.6 1.2 add_select_fusion.5
  92.8 1.2 add_select_fusion.5
  94.1 1.2 add_select_fusion.5
  95.3 1.2 add_select_fusion.5
  96.5 4.8 %fusion.106 = f32[7,128,512]{2,1,0:T(8,128)} fusion(f32[512,7,128]{0,2,1:T(8,128)} %bitcast.72, f32[7,128,128]{2,1,0:T(8,128)S(1)} %get-tuple-element.163, f32[7,128,128]{2,1,0:T(8,128)} %fusion.91), kind=kOutput, calls=%fused_computation.123 | convolution fusion | flops 704872448 | bytes 4587520 | tf_op jit(solution)/shard_map/nrhe,nhef->nrhf/dot_general | solution.py:99
  101.3 3.0 fusion.107
  104.2 18.6 %all-gather.5.cloned.1.call-done = f32[112,128,128]{2,1,0:T(8,128)} async-done(((f32[7,128,128]{2,1,0:T(8,128)}), f32[112,128,128]{2,1,0:T(8,128)}) %all-gather.5.cloned.1.call-update) | async-done | bytes 7340048 | tf_op jit(solution)/shard_map/all_gather | solution.py:17
  122.9 30.1 %while.28 = (s32[]{:T(128)}, f32[7,128,128]{2,1,0:T(8,128)}, s32[]{:T(128)}, f32[16,7,128,128]{3,2,1,0:T(8,128)}, s32[]{:T(128)}, /*index=5*/s32[]{:T(128)}) while((s32[]{:T(128)}, f32[7,128,128]{2,1,0:T(8,128)}, s32[]{:T(128)}, f32[16,7,128,128]{3,2,1,0:T(8,128)}, s32[]{:T(128)}, /*index=5*/s32[]{:T(128)}) %tuple.75), condition=%wide.region_1.0_spmd.clone, body=%wide.region_0.0_spmd.clone.sunk | while | flops 344068 | bytes 1376357 | solution.py:27
  122.9 1.9 add_select_fusion.4
  124.8 2.0 add_select_fusion.4
  126.7 2.0 add_select_fusion.4
  128.7 2.0 add_select_fusion.4
  130.7 2.0 add_select_fusion.4
  132.7 2.0 add_select_fusion.4
  134.6 2.0 add_select_fusion.4
  136.6 2.0 add_select_fusion.4
  138.6 2.0 add_select_fusion.4
  140.6 2.0 add_select_fusion.4
  142.5 2.0 add_select_fusion.4
  144.5 2.0 add_select_fusion.4
  146.5 2.0 add_select_fusion.4
  148.5 2.0 add_select_fusion.4
  150.5 2.0 add_select_fusion.4
  153.0 3.0 fusion.87
  156.0 3.0 fusion.105
  159.0 7.4 %multiply_add_fusion.1 = f32[7,128,512]{2,1,0:T(8,128)S(1)} fusion(f32[7,128,512]{2,1,0:T(8,128)S(1)} %copy-done.11, f32[512,7,128]{0,2,1:T(8,128)S(1)} %bitcast.69, f32[7,512,512]{2,1,0:T(8,128)} %fusion.89, f32[512,512]{1,0:T(8,128)S(1)} %fusion.94), kind=kOutput, calls=%fused_computation.95 | convolution fusion | flops 2821324800 | bytes 13893632 | tf_op jit(solution)/shard_map/nhrs,nrhe->nshe/dot_general | solution.py:83
  166.5 9.0 %add_multiply_fusion.1 = f32[7,128,512]{2,1,0:T(8,128)} fusion(f32[7,128,512]{2,1,0:T(8,128)S(1)} %fusion.87, f32[512,7,128]{0,2,1:T(8,128)S(1)} %bitcast.73, f32[7,512,512]{2,1,0:T(8,128)S(1)} %bitcast.56, f32[512,512]{1,0:T(8,128)S(1)} %fusion.94), kind=kOutput, calls=%fused_computation.97 | convolution fusion | flops 2821324800 | bytes 13893632 | tf_op jit(solution)/shard_map/nhrs,nshe->nrhe/dot_general | solution.py:82
  175.5 3.4 fusion.74
  178.9 2.2 copy.76
  181.1 4.5 %fusion.75 = bf16[1,512,896]{1,2,0:T(8,128)(2,1)} fusion(f32[7,128,512]{2,1,0:T(8,128)} %add_multiply_fusion.1, bf16[1,512,896]{1,2,0:T(8,128)(2,1)} %copy.63), kind=kLoop, calls=%fused_computation.93 | loop fusion | flops 17432576 | bytes 3670016 | tf_op jit(solution)/shard_map/convert_element_type | solution.py:106
  185.7 2.2 copy.75
  187.9 8.2 %multiply_add_fusion = f32[7,128,512]{2,1,0:T(8,128)S(1)} fusion(f32[7,128,512]{2,1,0:T(8,128)} %fusion.106, f32[7,512,512]{2,1,0:T(8,128)} %fusion.95, f32[512,512]{1,0:T(8,128)S(1)} %fusion.94, f32[512,7,128]{0,2,1:T(8,128)S(1)} %bitcast.60, f32[7,128]{1,0:T(8,128)S(1)} %bitcast.79), kind=kOutput, calls=%fused_computation.94 | convolution fusion | flops 2821783552 | bytes 13897216 | tf_op jit(solution)/shard_map/nhrs,nrhf->nshf/dot_general | solution.py:84
  196.1 3.3 fusion.73
  199.4 2.4 copy.77
  201.8 11.6 %fusion.72 = f32[7,128]{1,0:T(8,128)S(1)} fusion(f32[1,512,7,128]{1,3,2,0:T(8,128)S(1)} %bitcast.61, f32[7,128,512]{2,1,0:T(8,128)} %fusion.105, f32[512,7,128]{0,2,1:T(8,128)} %bitcast.63, f32[7,512,512]{2,1,0:T(8,128)} %fusion.95, f32[512,512]{1,0:T(8,128)S(1)} %fusion.94), kind=kOutput, calls=%fused_computation.87 | convolution fusion | flops 2822241280 | bytes 13897216 | tf_op jit(solution)/shard_map/nhrs,nshf->nrhf/dot_general | solution.py:81
  213.4 128.0 %psum.7 = f32[896]{0:T(1024)} all-reduce(f32[896]{0:T(1024)S(1)} %bitcast.80), channel_id=1, replica_groups=mesh['dp'=4,'head'=4,'ctx'=16] {'dp','ctx'}, use_global_device_ids=true, to_apply=%region_5.6 | all-reduce | flops 896 | bytes 7168 | tf_op jit(solution)/shard_map/psum | solution.py:103
  (47 shorter events, 2.8 us)
Async XLA Ops:
  7.2 64.3 %all-gather.7.cloned.1.call-start = ((), (), s32[]{:S(2)}) async-start(), calls=%async_computation.1 | async-start | bytes 7798784 | tf_op jit(solution)/shard_map/all_gather | solution.py:17
  11.7 3.0 copy-start.16
  13.5 1.3 copy-start.3
  17.5 105.3 %all-gather.5.cloned.1.call-start = ((), (), s32[]{:S(2)}) async-start(), calls=%async_computation | async-start | bytes 7798784 | tf_op jit(solution)/shard_map/all_gather | solution.py:17
  23.4 2.1 copy-start.9
  25.4 1.3 copy-start.5
  25.7 1.6 copy-start
  27.3 1.2 copy-start.14
  29.8 2.3 copy-start.15
  33.5 6.3 %copy-start.1 = (f32[1,512,896]{1,2,0:T(8,128)S(1)}, f32[1,512,896]{1,2,0:T(8,128)}, u32[]{:S(2)}) copy-start(f32[1,512,896]{1,2,0:T(8,128)} %copy-done) | copy-start | bytes 5505028
  96.5 4.8 %copy-start.2 = (f32[1,512,896]{1,2,0:T(8,128)S(1)}, f32[1,512,896]{1,2,0:T(8,128)}, u32[]{:S(2)}) copy-start(f32[1,512,896]{1,2,0:T(8,128)} %copy-done) | copy-start | bytes 5505028
  96.5 4.8 %copy-start.8 = (f32[7,128,128]{2,1,0:T(8,128)S(1)}, f32[7,128,128]{2,1,0:T(8,128)}, u32[]{:S(2)}) copy-start(f32[7,128,128]{2,1,0:T(8,128)} %fusion.91) | copy-start | bytes 1376260
  122.9 30.1 %copy-start.10 = (f32[7,128,128]{2,1,0:T(8,128)S(1)}, f32[7,128,128]{2,1,0:T(8,128)}, u32[]{:S(2)}) copy-start(f32[7,128,128]{2,1,0:T(8,128)} %fusion.97) | copy-start | bytes 1376260
  152.9 3.0 copy-start.4
  153.0 3.0 copy-start.7
  153.0 6.0 %copy-start.11 = (f32[7,128,512]{2,1,0:T(8,128)S(1)}, f32[7,128,512]{2,1,0:T(8,128)}, u32[]{:S(2)}) copy-start(f32[7,128,512]{2,1,0:T(8,128)} %fusion.107) | copy-start | bytes 5505028
  156.0 10.5 %slice-start = ((s8[7340032]{0:T(1024)(128)(4,1)}), s8[4194304]{0:T(1024)(128)(4,1)S(1)}, s32[]{:S(2)}) async-start(s8[7340032]{0:T(1024)(128)(4,1)} %bitcast.55), calls=%async_computation.2 | async-start | bytes 8388608
  159.0 7.5 %slice-start.1 = ((s8[7340032]{0:T(1024)(128)(4,1)}), s8[3145728]{0:T(1024)(128)(4,1)S(1)}, s32[]{:S(2)}) async-start(s8[7340032]{0:T(1024)(128)(4,1)} %bitcast.55), calls=%async_computation.3 | async-start | bytes 6291456
  159.0 7.5 %copy-start.6 = (f32[1,512,896]{1,2,0:T(8,128)S(1)}, f32[1,512,896]{1,2,0:T(8,128)}, u32[]{:S(2)}) copy-start(f32[1,512,896]{1,2,0:T(8,128)} %copy-done.5) | copy-start | bytes 5505028
  166.5 9.0 %copy-start.13 = (bf16[1,512,896]{1,2,0:T(8,128)(2,1)S(1)}, bf16[1,512,896]{1,2,0:T(8,128)(2,1)}, u32[]{:S(2)}) copy-start(bf16[1,512,896]{1,2,0:T(8,128)(2,1)} %copy.67) | copy-start | bytes 2752516
  187.9 8.2 %copy-start.12 = (bf16[1,512,896]{1,2,0:T(8,128)(2,1)S(1)}, bf16[1,512,896]{1,2,0:T(8,128)(2,1)}, u32[]{:S(2)}) copy-start(bf16[1,512,896]{1,2,0:T(8,128)(2,1)} %copy.72) | copy-start | bytes 2752516
Sparse Core Ops, SparseCore 0:
  17.7 53.7 all-gather.6
  73.3 49.5 all-gather.4
where the time goes:
time: 353 us; the launch traced here: 348 us
  blocking collectives  128 us (36%)
  matrix products  68.6 us (19%)
  other arithmetic  62.7 us (18%)
  waiting for transfers between devices  41.9 us (12%)
  local copies, waits for them, and re-layouts  31.5 us (9%)
  between operations  14.6 us (4%)
    psum x1, blocking collectives, per_device(): grad_gain = lax.psum(gain_local, ('dp', 'ctx'))  128 us
    select_n x30, other arithmetic, lap(): return jnp.where(position < mine, longer, running)  47.2 us
    all_gather x2, waiting for transfers between devices, entering(): pieces = lax.all_gather(value, axis)  41.9 us
    unnamed x48, local copies, waits for them, and re-layouts  24.5 us
    dot_general x1, matrix products, per_device(): jnp.einsum('nhrs,nshf->nrhf', scores, v_spike, precision=HIGHEST)  11.6 us
    convert_element_type x3, other arithmetic, finish(): (spike_grad.reshape(1, rows, width) * surrogate(pre)).astype(jnp.bfloat16)  11.3 us
    dot_general x1, matrix products, per_device(): jnp.einsum('nhrs,nshe->nrhe', weights, k_spike, precision=HIGHEST)  8.99 us
    dot_general x1, matrix products, per_device(): jnp.einsum('nrhf,nshf->nhrs', grad_out, v_spike, precision=HIGHEST) * causal  8.39 us
  transfers between devices with their start and end apart: 2, of which 2 were waited for; matrix products, arithmetic and copies ran while one was open for 17% of the time, Pallas kernels for 0%

commit v1 on v0

v1 whole, which is shorter than its diff:
```python
import math

import jax
import jax.numpy as jnp
from jax import lax
from jax.experimental import pallas as pl
from jax.experimental.pallas import tpu as pltpu
from jax.sharding import PartitionSpec as P

E = 128
SPIKE_STEPS = 4
F32 = jnp.float32
BF16 = jnp.bfloat16
UNIT = 8
CHUNK = 128


def spike(count):
    return ((count.astype(F32) - SPIKE_STEPS / 2) * 0.5).astype(BF16)


def mm(a, b, ca, cb):
    return lax.dot_general(a, b, (((ca,), (cb,)), ((), ())), preferred_element_type=F32)


def halves(x):
    hi = x.astype(BF16)
    return hi, (x - hi.astype(F32)).astype(BF16)


def surrogate(pre):
    w = pre.astype(F32) * (4.0 / math.log(2.0))
    c = jnp.exp2(w) + jnp.exp2(-w)
    b1, b2 = 2.0 * math.cosh(2.0), 2.0 * math.cosh(6.0)
    below = (c + b1) * (c + b2)
    r = pl.reciprocal(below, approx=True)
    r = r * (2.0 - below * r)
    n3 = 2.0 * (b1 + b2)
    n2 = 16.0 + 8.0 * b1 * b2
    n1 = 16.0 * (b1 + b2) + 2.0 * b1 * b2 * (b1 + b2)
    n0 = 8.0 * (b1 * b1 + b2 * b2)
    above = ((n3 * c + n2) * c + n1) * c + n0
    return (above * r) * r


def place():
    me = lax.axis_index("ctx")
    chip, core = me // 2, lax.rem(me, 2)
    return chip, core, 1 - 2 * core


def around(chip, steps, chips):
    return lax.rem(chip + steps + chips, chips)


def unit_list(chip, core, way, chips):
    units = []
    for k in range(1, chips // 2):
        shard = around(chip, way * k, chips)
        units += [2 * shard, 2 * shard + 1]
    return units + [2 * around(chip, chips // 2, chips) + core, 2 * chip + core]


def rows_of(unit):
    return pl.ds(pl.multiple_of(unit * UNIT, UNIT), UNIT)


def states_body(
    chips, heads, factor, q_ref, k_ref, v_ref, gy_ref,
    keep_ref, send_ref, qs_ref, ks_ref, vs_ref, gy_out, counts, both, sems,
):
    chip, core, way = place()
    mine = unit_list(chip, core, way, chips)
    other = unit_list(chip, 1 - core, -way, chips)
    copies = []
    for h in range(heads):
        lanes = slice(h * E, (h + 1) * E)
        pairs = [(ref.at[0, :, lanes], counts.at[i, :, lanes]) for i, ref in enumerate((q_ref, k_ref, v_ref))]
        pairs.append((gy_ref.at[0, :, lanes], gy_out.at[:, lanes]))
        copies.append([pltpu.make_async_copy(a, b, sems.at[i, h]) for i, (a, b) in enumerate(pairs)])
        for copy in copies[-1]:
            copy.start()
    for h in range(heads):
        lanes = slice(h * E, (h + 1) * E)
        for copy in copies[h]:
            copy.wait()
        q, k, v = (spike(counts[i, :, lanes]) for i in range(3))
        qs_ref[:, lanes] = q
        ks_ref[:, lanes] = k
        vs_ref[:, lanes] = v
        both[0, h] = mm(k, v, 0, 0)
        both[1, h] = factor * mm(q, gy_out[:, lanes], 0, 0)
    for i, (here, there) in enumerate(zip(mine, other)):
        for t in range(2):
            keep_ref[2 * i + t] = both[t, :, rows_of(here)]
            send_ref[2 * i + t] = both[t, :, rows_of(there)]
        send_ref[2 * len(mine) + i] = both[core, :, rows_of(here)]


def chip_body(chips, heads, keep_ref, got_ref, m1_ref, m2_ref, m3_ref, m4_ref, own_ref, g_ref):
    core = lax.rem(lax.axis_index("ctx"), 2)
    targets = [(m1_ref, 0), (m1_ref, 1), (m2_ref, 0), (m2_ref, 1), (m3_ref, 0), (m3_ref, 1)]
    targets += [(m4_ref, 0), (own_ref, 0)]
    cross = jnp.zeros((heads, UNIT, E), F32)
    for i, (ref, at) in enumerate(targets):
        kv, qd = keep_ref[2 * i], keep_ref[2 * i + 1]
        kv_got, qd_got = got_ref[2 * i], got_ref[2 * i + 1]
        ref[2 * at * heads : (2 * at + 1) * heads] = kv + kv_got
        ref[(2 * at + 1) * heads : (2 * at + 2) * heads] = qd + qd_got
        cross = cross + jnp.where(core == 0, kv * qd_got, kv_got * qd)
    g_ref[0] = jnp.zeros((UNIT, E), F32)
    g_ref[0, 0:heads] = jnp.sum(cross, axis=1)


def scan_body(chips, heads, x_ref, y_ref, o1_ref, o2_ref, o3_ref, o4_ref, own_ref, g_ref, have, give):
    chip, core, way = place()
    wide, near = 4 * heads, chips // 2
    for ref, go, lane in ((x_ref, way, core), (y_ref, -way, 1 - core)):
        for k in range(1, near):
            at = around(chip, -go * k, chips)
            have[at] = ref[wide * (k - 1) : wide * k].reshape(2, 2 * heads, UNIT, E)
        base = wide * (near - 1)
        have[around(chip, near, chips), lane] = ref[base : base + 2 * heads]
        have[chip, lane] = ref[base + 2 * heads : base + 4 * heads]
    zero = jnp.zeros((2, heads, UNIT, E), F32)
    before, after, cross = zero, zero, zero
    for i in range(chips):
        give[i, :, 0:heads] = before
        cross = cross + before * have[i, :, heads : 2 * heads]
        before = before + have[i, :, 0:heads]
    for i in reversed(range(chips)):
        give[i, :, heads : 2 * heads] = after
        after = after + have[i, :, heads : 2 * heads]
    last = wide * near
    g_ref[...] = x_ref[last : last + 1] + y_ref[last : last + 1]
    g_ref[0, 0:heads] = g_ref[0, 0:heads] + jnp.sum(cross[0] + cross[1], axis=1)
    for k, ref in ((1, o1_ref), (2, o2_ref), (3, o3_ref)):
        ref[0:wide] = give[around(chip, way * k, chips)].reshape(wide, UNIT, E)
        ref[wide : wide + 1] = g_ref[...]
    o4_ref[0 : 2 * heads] = give[around(chip, near, chips), core]
    o4_ref[2 * heads : 2 * heads + 1] = g_ref[...]
    own_ref[...] = give[chip].reshape(wide, UNIT, E)


def intra_body(heads, factor, qs_ref, ks_ref, vs_ref, gy_ref, gain_ref, dq_ref, dk_ref, dv_ref, g_ref):
    count = qs_ref.shape[0] // CHUNK
    first = lax.broadcasted_iota(jnp.int32, (CHUNK, CHUNK), 0)
    second = lax.broadcasted_iota(jnp.int32, (CHUNK, CHUNK), 1)
    lower, upper = first >= second, first <= second

    def twice(x, axis=1):
        return jnp.concatenate([x, x], axis=axis)

    def per_head(h, carry):
        lanes = pl.ds(pl.multiple_of(h * E, E), E)
        at = [slice(i * CHUNK, (i + 1) * CHUNK) for i in range(count)]
        q, k, v, gy = ([ref[rows, lanes] for rows in at] for ref in (qs_ref, ks_ref, vs_ref, gy_ref))
        gain = gain_ref[h]
        g_hi, g_lo = halves(gain)
        dq, dk, dv = [], [], []
        for i in range(count):
            vg = jnp.concatenate([v[i] * g_hi, v[i] * g_lo], axis=1)
            weights = jnp.where(lower, mm(twice(gy[i]), vg, 1, 1), 0.0)
            w_hi, w_lo = halves(weights)
            dq.append(mm(jnp.concatenate([w_hi, w_lo], axis=1), twice(k[i], 0), 1, 0))
            dk.append(mm(jnp.concatenate([w_hi, w_lo], axis=0), twice(q[i], 0), 0, 0))
            s_hi, s_lo = halves(jnp.where(upper, mm(k[i], q[i], 1, 1), 0.0))
            dv.append(mm(jnp.concatenate([s_hi, s_lo], axis=1), twice(gy[i], 0), 1, 0))
        state = None
        for i in range(count):
            if i > 0:
                kv = mm(k[i - 1], v[i - 1], 0, 0)
                state = kv if state is None else state + kv
                dq[i] += mm(twice(gy[i]), jnp.concatenate(halves(state * gain), axis=1), 1, 1)
            dq_ref[at[i], lanes] = factor * dq[i]
        state = None
        total = jnp.zeros((1, E), F32)
        for i in reversed(range(count)):
            if i + 1 < count:
                qd = mm(q[i + 1], gy[i + 1], 0, 0)
                state = qd if state is None else state + qd
                dk[i] += mm(twice(v[i]), jnp.concatenate(halves(state * gain), axis=1), 1, 1)
                dv[i] += mm(twice(k[i]), jnp.concatenate(halves(state), axis=0), 1, 0)
            dk_ref[at[i], lanes] = factor * dk[i]
            dv_plain = factor * dv[i]
            dv_ref[at[i], lanes] = dv_plain * gain
            total = total + jnp.sum(v[i].astype(F32) * dv_plain, axis=0, keepdims=True)
        g_ref[h] = total
        return carry

    lax.fori_loop(0, heads, per_head, 0)


def slope_body(q_ref, k_ref, v_ref, sq_ref, sk_ref, sv_ref):
    step = 32

    def some_rows(i, carry):
        rows = pl.ds(pl.multiple_of(i * step, step), step)
        for pre, out in ((q_ref, sq_ref), (k_ref, sk_ref), (v_ref, sv_ref)):
            out[rows] = surrogate(pre[0, rows])
        return carry

    lax.fori_loop(0, q_ref.shape[1] // step, some_rows, 0)


def finish_body(
    chips, heads, factor, u_ref, w_ref, own_ref, got_ref, gain_ref, gy_ref, ks_ref, vs_ref,
    dq_ref, dk_ref, dv_ref, sq_ref, sk_ref, sv_ref, oq_ref, ok_ref, ov_ref,
    state, stage, sems,
):
    chip, core, way = place()
    wide, near = 4 * heads, chips // 2
    tiles = wide + 1
    for ref, go, lane in ((u_ref, way, core), (w_ref, -way, 1 - core)):
        for k in range(1, near):
            shard = around(chip, -go * k, chips)
            for b in range(2):
                for t in range(2):
                    base = tiles * (k - 1) + (2 * b + t) * heads
                    state[t, :, rows_of(2 * shard + b)] = ref[base : base + heads]
        for t in range(2):
            base = tiles * (near - 1) + t * heads
            unit = 2 * around(chip, near, chips) + lane
            state[t, :, rows_of(unit)] = ref[base : base + heads]
    for b in range(2):
        for t in range(2):
            base = (2 * b + t) * heads
            state[t, :, rows_of(2 * chip + b)] = own_ref[base : base + heads]
    kind = 1 - core
    mine = unit_list(chip, core, way, chips)
    other = unit_list(chip, 1 - core, -way, chips)
    for i, (here, there) in enumerate(zip(mine, other)):
        state[kind, :, rows_of(here)] += got_ref[2 * i + kind]
        state[kind, :, rows_of(there)] += got_ref[2 * len(mine) + i]
    copies = []
    for h in range(heads):
        lanes = slice(h * E, (h + 1) * E)
        gain = gain_ref[h]
        gy, k, v = gy_ref[:, lanes], ks_ref[:, lanes], vs_ref[:, lanes]
        m2 = jnp.concatenate(halves(state[0, h] * (gain * factor)), axis=1)
        g_hi, g_lo = halves(state[1, h] * gain)
        dq = dq_ref[:, lanes] + mm(jnp.concatenate([gy, gy], axis=1), m2, 1, 1)
        stage[0, :, lanes] = (dq * sq_ref[:, lanes]).astype(BF16)
        dk = dk_ref[:, lanes] + mm(
            jnp.concatenate([v, v], axis=1), jnp.concatenate([g_hi, g_lo], axis=1), 1, 1
        )
        stage[1, :, lanes] = (dk * sk_ref[:, lanes]).astype(BF16)
        dv = dv_ref[:, lanes] + mm(
            jnp.concatenate([k, k], axis=1), jnp.concatenate([g_hi, g_lo], axis=0), 1, 0
        )
        stage[2, :, lanes] = (dv * sv_ref[:, lanes]).astype(BF16)
        for i, out in enumerate((oq_ref, ok_ref, ov_ref)):
            copy = pltpu.make_async_copy(stage.at[i, :, lanes], out.at[0, :, lanes], sems.at[i, h])
            copy.start()
            copies.append(copy)
    for copy in copies:
        copy.wait()


def params(mib, **more):
    return pltpu.CompilerParams(vmem_limit_bytes=mib * 1024 * 1024, **more)


def cost(us):
    return pl.CostEstimate(flops=int(us * 1e9), bytes_accessed=int(us * 2e6), transcendentals=0)


def per_device(q_count, k_count, v_count, q_pre, k_pre, v_pre, grad_y, gain):
    rows, width = q_count.shape[1], q_count.shape[2]
    heads = width // E
    devices = lax.axis_size("ctx")
    chips = devices // 2
    near = chips // 2
    factor = 1.0 / math.sqrt(E * rows * devices)
    units = E // UNIT
    assert units == devices and near == 4
    gain_h = gain.reshape(heads, 1, E)

    def shape(*dims, dtype=F32):
        return jax.ShapeDtypeStruct(dims, dtype)

    def tiles(count):
        return shape(count, UNIT, E)

    swap = [(i, i ^ 1) for i in range(devices)]

    def ring(k):
        pairs = []
        for z in range(chips):
            pairs.append((2 * z, 2 * ((z + k) % chips)))
            pairs.append((2 * z + 1, 2 * ((z - k) % chips) + 1))
        return pairs

    def exchange(parts):
        return [lax.ppermute(part, "ctx", ring(k)) for k, part in enumerate(parts, 1)]

    with jax.named_scope("local_states"):
        keep, send, q_spike, k_spike, v_spike, gy = pl.pallas_call(
            lambda *refs: states_body(chips, heads, factor, *refs),
            in_specs=[pl.BlockSpec(memory_space=pltpu.HBM)] * 4,
            out_shape=[shape(units, heads, UNIT, E), shape(units * 3 // 2, heads, UNIT, E)]
            + [shape(rows, width, dtype=BF16)] * 4,
            scratch_shapes=[
                pltpu.VMEM((3, rows, width), jnp.int32),
                pltpu.VMEM((2, heads, E, E), F32),
                pltpu.SemaphoreType.DMA((4, heads)),
            ],
            compiler_params=params(9),
            cost_estimate=cost(3),
            name="local_states",
        )(*(pltpu.with_memory_space_constraint(x, pltpu.HBM) for x in (q_count, k_count, v_count, grad_y)))
        got = lax.ppermute(send, "ctx", swap)

    with jax.named_scope("chip_states"):
        *parts, own, g_chip = pl.pallas_call(
            lambda *refs: chip_body(chips, heads, *refs),
            out_shape=[tiles(4 * heads)] * 3 + [tiles(2 * heads)] * 2 + [tiles(1)],
            compiler_params=params(2),
            name="chip_states",
        )(keep, got)

    with jax.named_scope("to_owners"):
        parts = exchange(parts)

    with jax.named_scope("intra"):
        gain_late, parts[0] = lax.optimization_barrier((gain_h, parts[0]))
        dq, dk, dv, g_intra = pl.pallas_call(
            lambda *refs: intra_body(heads, factor, *refs),
            out_shape=[shape(rows, width)] * 3 + [shape(heads, 1, E)],
            compiler_params=params(4),
            cost_estimate=cost(7),
            name="intra",
        )(q_spike, k_spike, v_spike, gy, gain_late)

    with jax.named_scope("to_core"):
        g_mine = g_chip + jnp.pad(g_intra.reshape(1, heads, E), ((0, 0), (0, UNIT - heads), (0, 0)))
        pack = jnp.concatenate([*parts, own, g_mine])
        pack_got = lax.ppermute(pack, "ctx", swap)

    with jax.named_scope("scan"):
        *parts, own, g_all = pl.pallas_call(
            lambda *refs: scan_body(chips, heads, *refs),
            out_shape=[tiles(4 * heads + 1)] * 3 + [tiles(2 * heads + 1), tiles(4 * heads), tiles(1)],
            scratch_shapes=[pltpu.VMEM((chips, 2, 2 * heads, UNIT, E), F32)] * 2,
            compiler_params=params(4),
            name="scan",
        )(pack, pack_got)

    with jax.named_scope("from_owners"):
        parts = exchange(parts)

    with jax.named_scope("slopes"):
        *late, parts[0] = lax.optimization_barrier((q_pre, k_pre, v_pre, parts[0]))
        sq, sk, sv = pl.pallas_call(
            slope_body,
            out_shape=[shape(rows, width)] * 3,
            compiler_params=params(2),
            cost_estimate=cost(5),
            name="slopes",
        )(*late)

    with jax.named_scope("states"):
        sq, *parts = lax.optimization_barrier((sq, *parts))
        mine = jnp.concatenate(parts)
        theirs = lax.ppermute(mine, "ctx", swap)

    with jax.named_scope("grad_gain"):
        lasts = [(4 * heads + 1) * (i + 1) - 1 for i in range(near - 1)]
        g_sum = g_all + mine[-1:]
        for i in lasts:
            g_sum = g_sum + mine[i : i + 1] + theirs[i : i + 1]
        size = lax.axis_size("dp")
        total = g_sum
        for step in range(1, size):
            total = total + lax.ppermute(
                g_sum, "dp", [(i, (i + step) % size) for i in range(size)]
            )
        grad_gain = total[0, :heads].reshape(width)

    with jax.named_scope("finish"):
        whole = pl.BlockSpec(memory_space=pltpu.VMEM)
        grads = pl.pallas_call(
            lambda *refs: finish_body(chips, heads, factor, *refs),
            in_specs=[whole] * 14,
            out_specs=[pl.BlockSpec(memory_space=pl.ANY)] * 3,
            out_shape=[shape(1, rows, width, dtype=BF16)] * 3,
            scratch_shapes=[
                pltpu.VMEM((2, heads, E, E), F32),
                pltpu.VMEM((3, rows, width), BF16),
                pltpu.SemaphoreType.DMA((3, heads)),
            ],
            compiler_params=params(8),
            name="finish",
        )(mine, theirs, own, got, gain_h, gy, k_spike, v_spike, dq, dk, dv, sq, sk, sv)
    return (*grads, grad_gain)


def solution(mesh):
    placed = P("dp", "ctx", "head")
    return jax.shard_map(
        per_device,
        mesh=mesh,
        in_specs=(placed,) * 7 + (P("head"),),
        out_specs=(placed,) * 3 + (P("head"),),
        check_vma=False,
    )
```

time: 353 us -> 62.1 us (0.18); the launches traced: 348 us -> 61.6 us
  blocking collectives: 128 us -> 0 us
  matrix products: 68.6 us -> 0 us
  other arithmetic: 62.7 us -> 0.02 us
  waiting for transfers between devices: 41.9 us -> 7.95 us
  local copies, waits for them, and re-layouts: 31.5 us -> 3.61 us
  starting transfers between devices: 0.37 us -> 27.1 us
  Pallas kernels: 0 us -> 22.1 us
  between operations: 14.6 us -> 0.87 us
    psum x1 -> x0, blocking collectives: 128 us -> none  [per_device(): grad_gain = lax.psum(gain_local, ('dp', 'ctx'))]
    dot_general x12 -> x0, matrix products: 68.6 us -> none  [the longest x1 11.6 us: per_device(): jnp.einsum('nhrs,nshf->nrhf', scores, v_spike, precision=HIGHEST)]
    select_n x30 -> x0, other arithmetic: 47.2 us -> none  [lap(): return jnp.where(position < mine, longer, running)]
    all_gather x2 -> x0, waiting for transfers between devices: 41.9 us -> none  [entering(): pieces = lax.all_gather(value, axis)]
    ppermute x0 -> x14, starting transfers between devices: none -> 27.1 us  [the longest x8 19.1 us: exchange(): lax.ppermute(part, 'ctx', ring(k))]
    pallas_call x0 -> x6, Pallas kernels: none -> 22.1 us  [the longest x1 10.5 us: per_device(): pl.pallas_call(lambda *refs: intra_body(heads, factor, *refs), out_shape=...]
    unnamed x48 -> x26, local copies, waits for them, and re-layouts: 24.5 us -> 3 us
    convert_element_type x5 -> x0, other arithmetic: 11.6 us -> none  [the longest x3 11.3 us: finish(): (spike_grad.reshape(1, rows, width) * surrogate(pre)).astype(jnp.bfloat16)]
  transfers between devices with their start and end apart: 2 -> 14, of which waited for: 2 -> 4; matrix products, arithmetic and copies ran while one was open for 17% -> 2% of each run, Pallas kernels for 0% -> 28%
where the time goes in v1:
time: 62.1 us; the launch traced here: 61.6 us
  starting transfers between devices  27.1 us (44%)
  Pallas kernels  22.1 us (36%)
  waiting for transfers between devices  7.95 us (13%)
  local copies, waits for them, and re-layouts  3.61 us (6%)
  between operations  0.87 us (1%)
    ppermute x8, starting transfers between devices, exchange(): lax.ppermute(part, 'ctx', ring(k))  19.1 us
    pallas_call x1, Pallas kernels, per_device(): pl.pallas_call(lambda *refs: intra_body(heads, factor, *refs), out_shape=...  10.5 us
    ppermute x3, starting transfers between devices, per_device(): lax.ppermute(g_sum, 'dp', [(i, (i + step) % size) for i in range(size)])  5.67 us
    pallas_call x1, Pallas kernels, per_device(): pl.pallas_call(slope_body, out_shape=[shape(rows, width)] * 3, compiler_p...  3.92 us
    pallas_call x1, Pallas kernels, per_device(): pl.pallas_call(lambda *refs: states_body(chips, heads, factor, *refs), in...  3.79 us
    unnamed x26, local copies, waits for them, and re-layouts  3 us
    pallas_call x1, Pallas kernels, per_device(): pl.pallas_call(lambda *refs: finish_body(chips, heads, factor, *refs), in...  2.97 us
    ppermute x8, waiting for transfers between devices, exchange(): lax.ppermute(part, 'ctx', ring(k))  2.61 us
  transfers between devices with their start and end apart: 14, of which 4 were waited for; matrix products, arithmetic and copies ran while one was open for 2% of the time, Pallas kernels for 28%

profile of v1, /device:TPU:16, one launch (start us, length us, event | category | flops | bytes accessed | tf_op | source)
XLA Modules:
  0.0 61.6 jit_solution(5178007081752516558)
XLA Ops:
  0.6 0.0 copy-start.8
  0.6 3.8 %local_states.1 = (f32[16,7,8,128]{3,2,1,0:T(8,128)S(1)}, f32[24,7,8,128]{3,2,1,0:T(8,128)S(1)}, bf16[512,896]{1,0:T(8,128)(2,1)S(1)}, bf16[512,896]{1,0:T(8,128...) custom-call(s32[1,512,896]{2,1,0:T(8,128)} %refs_0_.1, s32[1,512,896]{2,1,0:T(8,128)} %refs_1_.1, ...), custom_call_target="tpu_custom_call" | custom-call | flops 3000000000 | bytes 6000000 | tf_op jit(solution)/shard_map/local_states/local_states/pallas_call | solution.py:298
  4.4 0.0 copy-start.6
  4.5 0.1 collective-permute-start
  4.6 2.1 %collective-permute-done.refs_1_.refs_3_ = f32[24,7,8,128]{3,2,1,0:T(8,128)S(1)} collective-permute-done((f32[24,7,8,128]{3,2,1,0:T(8,128)S(1)}, f32[24,7,8,128]{3,2,1,0:T(8,128)S(1)}, u32[]{:S(2)}, u32[]{:S(2)}) %collective-permute-start) | collective-permute-done | bytes 688160 | tf_op jit(solution)/shard_map/local_states/ppermute | solution.py:312
  6.7 0.7 %chip_states.1 = (f32[28,8,128]{2,1,0:T(8,128)}, f32[28,8,128]{2,1,0:T(8,128)S(1)}, f32[28,8,128]{2,1,0:T(8,128)S(1)}, f32[14,8,128]{2,1,0:T(8,128)S(1)}, f32[14...) custom-call(f32[16,7,8,128]{3,2,1,0:T(8,128)S(1)} %get-tuple-element.43.refs_0_, ...), custom_call_target="tpu_custom_call" | custom-call | tf_op jit(solution)/shard_map/chip_states/chip_states/pallas_call | solution.py:315
  7.4 0.0 copy-start.3
  7.4 0.0 copy-start.4
  7.4 0.0 copy-start.5
  7.4 0.0 copy-done.6
  7.4 0.6 %copy-done.3 = f32[28,8,128]{2,1,0:T(8,128)} copy-done((f32[28,8,128]{2,1,0:T(8,128)}, f32[28,8,128]{2,1,0:T(8,128)S(1)}, u32[]{:S(2)}) %copy-start.3) | copy-done | bytes 114712
  8.0 0.0 copy-done.4
  8.1 0.0 copy-done.5
  8.1 1.9 %collective-permute-start.1 = (f32[28,8,128]{2,1,0:T(8,128)}, f32[28,8,128]{2,1,0:T(8,128)}, u32[]{:S(2)}, u32[]{:S(2)}) collective-permute-start(f32[28,8,128]{2,1,0:T(8,128)} %get-tuple-element.45), channel_id=1, source_target_pairs={{0,2},{1,15},{2,4},{3,1},{4,6},{5,3},{6,8},{7,5},{8,10},{9,7},{10,... | collective-permute-start | bytes 344072 | tf_op jit(solution)/shard_map/to_owners/ppermute | solution.py:295
  10.0 0.0 copy-done.8
  10.0 3.3 %collective-permute-start.2 = (f32[28,8,128]{2,1,0:T(8,128)}, f32[28,8,128]{2,1,0:T(8,128)S(1)}, u32[]{:S(2)}, u32[]{:S(2)}) collective-permute-start(f32[28,8,128]{2,1,0:T(8,128)} %copy-done.4), channel_id=1, source_target_pairs={{0,4},{1,13},{2,6},{3,15},{4,8},{5,1},{6,10},{7,3},{8,12},{9,5},{1... | collective-permute-start | bytes 344072 | tf_op jit(solution)/shard_map/to_owners/ppermute | solution.py:295
  13.3 4.0 %collective-permute-start.3 = (f32[28,8,128]{2,1,0:T(8,128)}, f32[28,8,128]{2,1,0:T(8,128)S(1)}, u32[]{:S(2)}, u32[]{:S(2)}) collective-permute-start(f32[28,8,128]{2,1,0:T(8,128)} %copy-done.3), channel_id=1, source_target_pairs={{0,6},{1,11},{2,8},{3,13},{4,10},{5,15},{6,12},{7,1},{8,14},{9,3},... | collective-permute-start | bytes 344072 | tf_op jit(solution)/shard_map/to_owners/ppermute | solution.py:295
  17.3 0.5 collective-permute-start.4
  17.9 0.0 collective-permute-done.1
  17.9 0.0 copy-start.7
  17.9 1.2 %copy-done.7 = bf16[512,896]{1,0:T(8,128)(2,1)S(1)} copy-done((bf16[512,896]{1,0:T(8,128)(2,1)S(1)}, bf16[512,896]{1,0:T(8,128)(2,1)}, u32[]{:S(2)}) %copy-start.7) | copy-done | bytes 917528
  19.0 0.0 copy-start.2
  19.0 10.5 %intra.1 = (f32[512,896]{1,0:T(8,128)S(1)}, f32[512,896]{1,0:T(8,128)S(1)}, f32[512,896]{1,0:T(8,128)S(1)}, f32[7,1,128]{2,1,0:T(1,128)S(1)}) custom-call(bf16[512,896]{1,0:T(8,128)(2,1)S(1)} %copy-done.7, bf16[512,896]{1,0:T(8,128)(2,1)S(1)} %get-tuple-element.53.refs_1_.refs_6_, bf16[512,896]{1,0:T(8,128)(2,1)S(1)} %get-tuple-element.54.refs_2_.refs_7_, ...), custom_call_target="tpu_custom_call" | custom-call | flops 7000000000 | bytes 14000000 | tf_op jit(solution)/shard_map/intra/intra/pallas_call | solution.py:327
  29.5 0.0 copy-start
  29.6 0.0 copy-start.1
  29.6 1.0 %constant_dynamic-update-slice_fusion.5 = f32[113,8,128]{2,1,0:T(8,128)S(1)} fusion(f32[28,8,128]{2,1,0:T(8,128)} %collective-permute-done.1), kind=kLoop, calls=%fused_computation.5 | loop fusion | bytes 229376
  30.6 0.0 collective-permute-done.2
  30.6 0.0 collective-permute-done.3
  30.7 0.0 collective-permute-done.4
  30.7 2.1 %collective-permute-start.5 = (f32[113,8,128]{2,1,0:T(8,128)S(1)}, f32[113,8,128]{2,1,0:T(8,128)S(1)}, u32[]{:S(2)}, u32[]{:S(2)}) collective-permute-start(f32[113,8,128]{2,1,0:T(8,128)S(1)} %constant_dynamic-update-slice_fusion.refs_0_), channel_id=1, source_target_pairs={{0,1},{1,0},{2,3},{3,2},{4,5},{5,4},{6,7},{7,6},{8,9},{9,8},{10,11... | collective-permute-start | bytes 1388552 | tf_op jit(solution)/shard_map/to_core/ppermute | solution.py:338
  32.9 1.4 %collective-permute-done.5.refs_1_ = f32[113,8,128]{2,1,0:T(8,128)S(1)} collective-permute-done((f32[113,8,128]{2,1,0:T(8,128)S(1)}, f32[113,8,128]{2,1,0:T(8,128)S(1)}, u32[]{:S(2)}, u32[]{:S(2)}) %collective-permute-start.5) | collective-permute-done | bytes 462880 | tf_op jit(solution)/shard_map/to_core/ppermute | solution.py:338
  34.3 0.2 scan.1
  34.5 1.1 %collective-permute-start.6 = (f32[29,8,128]{2,1,0:T(8,128)S(1)}, f32[29,8,128]{2,1,0:T(8,128)S(1)}, u32[]{:S(2)}, u32[]{:S(2)}) collective-permute-start(f32[29,8,128]{2,1,0:T(8,128)S(1)} %get-tuple-element.58), channel_id=1, source_target_pairs={{0,2},{1,15},{2,4},{3,1},{4,6},{5,3},{6,8},{7,5},{8,10},{9,7},{10,... | collective-permute-start | bytes 356360 | tf_op jit(solution)/shard_map/from_owners/ppermute | solution.py:295
  35.6 2.8 %collective-permute-start.7 = (f32[29,8,128]{2,1,0:T(8,128)S(1)}, f32[29,8,128]{2,1,0:T(8,128)S(1)}, u32[]{:S(2)}, u32[]{:S(2)}) collective-permute-start(f32[29,8,128]{2,1,0:T(8,128)S(1)} %get-tuple-element.64), channel_id=1, source_target_pairs={{0,4},{1,13},{2,6},{3,15},{4,8},{5,1},{6,10},{7,3},{8,12},{9,5},{1... | collective-permute-start | bytes 356360 | tf_op jit(solution)/shard_map/from_owners/ppermute | solution.py:295
  38.4 1.0 %collective-permute-start.8 = (f32[29,8,128]{2,1,0:T(8,128)S(1)}, f32[29,8,128]{2,1,0:T(8,128)S(1)}, u32[]{:S(2)}, u32[]{:S(2)}) collective-permute-start(f32[29,8,128]{2,1,0:T(8,128)S(1)} %get-tuple-element.65), channel_id=1, source_target_pairs={{0,6},{1,11},{2,8},{3,13},{4,10},{5,15},{6,12},{7,1},{8,14},{9,3},... | collective-permute-start | bytes 356360 | tf_op jit(solution)/shard_map/from_owners/ppermute | solution.py:295
  39.4 4.5 %collective-permute-start.9 = (f32[15,8,128]{2,1,0:T(8,128)S(1)}, f32[15,8,128]{2,1,0:T(8,128)S(1)}, u32[]{:S(2)}, u32[]{:S(2)}) collective-permute-start(f32[15,8,128]{2,1,0:T(8,128)S(1)} %get-tuple-element.66), channel_id=1, source_target_pairs={{0,8},{1,9},{2,10},{3,11},{4,12},{5,13},{6,14},{7,15},{8,0},{9,1},... | collective-permute-start | bytes 184328 | tf_op jit(solution)/shard_map/from_owners/ppermute | solution.py:295
  43.9 0.0 collective-permute-done.6
  43.9 0.0 copy-done.2
  43.9 0.0 copy-done
  43.9 0.0 copy-done.1
  43.9 3.9 %slopes.1 = (f32[512,896]{1,0:T(8,128)S(1)}, f32[512,896]{1,0:T(8,128)S(1)}, f32[512,896]{1,0:T(8,128)S(1)}) custom-call(bf16[1,512,896]{2,1,0:T(8,128)(2,1)S(1)} %copy-done, bf16[1,512,896]{2,1,0:T(8,128)(2,1)S(1)} %copy-done.1, bf16[1,512,896]{2,1,0:T(8,128)(2,1)S(1)} %copy-done.2), custom_call_target="tpu_custom_call" | custom-call | flops 5000000000 | bytes 10000000 | tf_op jit(solution)/shard_map/slopes/slopes/pallas_call | solution.py:354
  47.8 2.6 %collective-permute-done.9 = f32[15,8,128]{2,1,0:T(8,128)S(1)} collective-permute-done((f32[15,8,128]{2,1,0:T(8,128)S(1)}, f32[15,8,128]{2,1,0:T(8,128)S(1)}, u32[]{:S(2)}, u32[]{:S(2)}) %collective-permute-start.9) | collective-permute-done | bytes 61472 | tf_op jit(solution)/shard_map/from_owners/ppermute | solution.py:295
  50.4 0.0 collective-permute-done.7
  50.4 0.0 collective-permute-done.8
  50.5 0.1 collective-permute-start.10
  50.6 1.7 %collective-permute-done.10.refs_1_ = f32[102,8,128]{2,1,0:T(8,128)S(1)} collective-permute-done((f32[102,8,128]{2,1,0:T(8,128)S(1)}, f32[102,8,128]{2,1,0:T(8,128)S(1)}, u32[]{:S(2)}, u32[]{:S(2)}) %collective-permute-start.10) | collective-permute-done | bytes 417824 | tf_op jit(solution)/shard_map/states/ppermute | solution.py:365
  52.4 1.7 %collective-permute-start.11 = (f32[1,8,128]{2,1,0:T(8,128)S(1)}, f32[1,8,128]{2,1,0:T(8,128)S(1)}, u32[]{:S(2)}, u32[]{:S(2)}) collective-permute-start(f32[1,8,128]{2,1,0:T(8,128)S(1)} %slice_add_fusion), channel_id=1, source_target_pairs={{0,64},{64,128},{128,192},{192,0},{1,65},{65,129},{129,193},{193,1... | collective-permute-start | bytes 12296 | tf_op jit(solution)/shard_map/grad_gain/ppermute | solution.py:375
  54.0 2.6 %collective-permute-start.12 = (f32[1,8,128]{2,1,0:T(8,128)S(1)}, f32[1,8,128]{2,1,0:T(8,128)S(1)}, u32[]{:S(2)}, u32[]{:S(2)}) collective-permute-start(f32[1,8,128]{2,1,0:T(8,128)S(1)} %slice_add_fusion), channel_id=1, source_target_pairs={{0,128},{64,192},{128,0},{192,64},{1,129},{65,193},{129,1},{193,65... | collective-permute-start | bytes 12296 | tf_op jit(solution)/shard_map/grad_gain/ppermute | solution.py:375
  56.6 1.4 %collective-permute-start.13 = (f32[1,8,128]{2,1,0:T(8,128)S(1)}, f32[1,8,128]{2,1,0:T(8,128)S(1)}, u32[]{:S(2)}, u32[]{:S(2)}) collective-permute-start(f32[1,8,128]{2,1,0:T(8,128)S(1)} %slice_add_fusion), channel_id=1, source_target_pairs={{0,192},{64,0},{128,64},{192,128},{1,193},{65,1},{129,65},{193,129... | collective-permute-start | bytes 12296 | tf_op jit(solution)/shard_map/grad_gain/ppermute | solution.py:375
  58.0 3.0 %finish.1 = (bf16[1,512,896]{2,1,0:T(8,128)(2,1)}, bf16[1,512,896]{2,1,0:T(8,128)(2,1)}, bf16[1,512,896]{2,1,0:T(8,128)(2,1)}) custom-call(f32[102,8,128]{2,1,0:T(8,128)S(1)} %constant_dynamic-update-slice_fusion.6.refs_0_, f32[102,8,128]{2,1,0:T(8,128)S(1)} %collective-permute-done.10.refs_1_, f32[28,8,128]{2,1,0:T(8,128)S(1)} %get-tuple-element.71.refs_2_, ...), custom_call_target="tpu_custom_call" | custom-call | tf_op jit(solution)/shard_map/finish/finish/pallas_call | solution.py:382
  61.0 0.0 collective-permute-done.11
  61.0 0.0 collective-permute-done.12
  61.0 0.0 collective-permute-done.13
  61.0 0.6 slice_bitcast_fusion
  (13 shorter events, 0.1 us)
Async XLA Ops:
  0.6 9.4 %copy-start.8 = (f32[896]{0:T(1024)S(1)}, f32[896]{0:T(1024)}, u32[]{:S(2)}) copy-start(f32[896]{0:T(1024)} %param.15) | copy-start | bytes 10756
  4.4 2.9 %copy-start.6 = (bf16[512,896]{1,0:T(8,128)(2,1)}, bf16[512,896]{1,0:T(8,128)(2,1)S(1)}, u32[]{:S(2)}) copy-start(bf16[512,896]{1,0:T(8,128)(2,1)S(1)} %get-tuple-element.52.refs_0_) | copy-start | bytes 2752516
  4.5 2.2 %collective-permute-start = (f32[24,7,8,128]{3,2,1,0:T(8,128)S(1)}, f32[24,7,8,128]{3,2,1,0:T(8,128)S(1)}, u32[]{:S(2)}, u32[]{:S(2)}) collective-permute-start(f32[24,7,8,128]{3,2,1,0:T(8,128)S(1)} %get-tuple-element.44), channel_id=1, source_target_pairs={{0,1},{1,0},{2,3},{3,2},{4,5},{5,4},{6,7},{7,6},{8,9},{9,8},{10,11... | collective-permute-start | bytes 2064392 | tf_op jit(solution)/shard_map/local_states/ppermute | solution.py:312
  7.4 0.6 %copy-start.3 = (f32[28,8,128]{2,1,0:T(8,128)}, f32[28,8,128]{2,1,0:T(8,128)S(1)}, u32[]{:S(2)}) copy-start(f32[28,8,128]{2,1,0:T(8,128)S(1)} %get-tuple-element.48) | copy-start | bytes 344068
  7.4 0.7 %copy-start.4 = (f32[28,8,128]{2,1,0:T(8,128)}, f32[28,8,128]{2,1,0:T(8,128)S(1)}, u32[]{:S(2)}) copy-start(f32[28,8,128]{2,1,0:T(8,128)S(1)} %get-tuple-element.47) | copy-start | bytes 344068
  7.4 0.7 %copy-start.5 = (f32[14,8,128]{2,1,0:T(8,128)}, f32[14,8,128]{2,1,0:T(8,128)S(1)}, u32[]{:S(2)}) copy-start(f32[14,8,128]{2,1,0:T(8,128)S(1)} %get-tuple-element.49) | copy-start | bytes 172036
  8.1 9.8 %collective-permute-start.1 = (f32[28,8,128]{2,1,0:T(8,128)}, f32[28,8,128]{2,1,0:T(8,128)}, u32[]{:S(2)}, u32[]{:S(2)}) collective-permute-start(f32[28,8,128]{2,1,0:T(8,128)} %get-tuple-element.45), channel_id=1, source_target_pairs={{0,2},{1,15},{2,4},{3,1},{4,6},{5,3},{6,8},{7,5},{8,10},{9,7},{10,... | collective-permute-start | bytes 344072 | tf_op jit(solution)/shard_map/to_owners/ppermute | solution.py:295
  10.0 20.6 %collective-permute-start.2 = (f32[28,8,128]{2,1,0:T(8,128)}, f32[28,8,128]{2,1,0:T(8,128)S(1)}, u32[]{:S(2)}, u32[]{:S(2)}) collective-permute-start(f32[28,8,128]{2,1,0:T(8,128)} %copy-done.4), channel_id=1, source_target_pairs={{0,4},{1,13},{2,6},{3,15},{4,8},{5,1},{6,10},{7,3},{8,12},{9,5},{1... | collective-permute-start | bytes 344072 | tf_op jit(solution)/shard_map/to_owners/ppermute | solution.py:295
  13.3 17.4 %collective-permute-start.3 = (f32[28,8,128]{2,1,0:T(8,128)}, f32[28,8,128]{2,1,0:T(8,128)S(1)}, u32[]{:S(2)}, u32[]{:S(2)}) collective-permute-start(f32[28,8,128]{2,1,0:T(8,128)} %copy-done.3), channel_id=1, source_target_pairs={{0,6},{1,11},{2,8},{3,13},{4,10},{5,15},{6,12},{7,1},{8,14},{9,3},... | collective-permute-start | bytes 344072 | tf_op jit(solution)/shard_map/to_owners/ppermute | solution.py:295
  17.3 13.4 %collective-permute-start.4 = (f32[14,8,128]{2,1,0:T(8,128)}, f32[14,8,128]{2,1,0:T(8,128)S(1)}, u32[]{:S(2)}, u32[]{:S(2)}) collective-permute-start(f32[14,8,128]{2,1,0:T(8,128)} %copy-done.5), channel_id=1, source_target_pairs={{0,8},{1,9},{2,10},{3,11},{4,12},{5,13},{6,14},{7,15},{8,0},{9,1},... | collective-permute-start | bytes 172040 | tf_op jit(solution)/shard_map/to_owners/ppermute | solution.py:295
  17.9 1.2 %copy-start.7 = (bf16[512,896]{1,0:T(8,128)(2,1)S(1)}, bf16[512,896]{1,0:T(8,128)(2,1)}, u32[]{:S(2)}) copy-start(bf16[512,896]{1,0:T(8,128)(2,1)} %copy-done.6) | copy-start | bytes 2752516
  19.0 24.9 %copy-start.2 = (bf16[1,512,896]{2,1,0:T(8,128)(2,1)S(1)}, bf16[1,512,896]{2,1,0:T(8,128)(2,1)}, u32[]{:S(2)}) copy-start(bf16[1,512,896]{2,1,0:T(8,128)(2,1)} %v_ref) | copy-start | bytes 2752516
  29.5 14.4 %copy-start = (bf16[1,512,896]{2,1,0:T(8,128)(2,1)S(1)}, bf16[1,512,896]{2,1,0:T(8,128)(2,1)}, u32[]{:S(2)}) copy-start(bf16[1,512,896]{2,1,0:T(8,128)(2,1)} %q_ref) | copy-start | bytes 2752516
  29.6 14.3 %copy-start.1 = (bf16[1,512,896]{2,1,0:T(8,128)(2,1)S(1)}, bf16[1,512,896]{2,1,0:T(8,128)(2,1)}, u32[]{:S(2)}) copy-start(bf16[1,512,896]{2,1,0:T(8,128)(2,1)} %k_ref) | copy-start | bytes 2752516
  30.7 3.6 %collective-permute-start.5 = (f32[113,8,128]{2,1,0:T(8,128)S(1)}, f32[113,8,128]{2,1,0:T(8,128)S(1)}, u32[]{:S(2)}, u32[]{:S(2)}) collective-permute-start(f32[113,8,128]{2,1,0:T(8,128)S(1)} %constant_dynamic-update-slice_fusion.refs_0_), channel_id=1, source_target_pairs={{0,1},{1,0},{2,3},{3,2},{4,5},{5,4},{6,7},{7,6},{8,9},{9,8},{10,11... | collective-permute-start | bytes 1388552 | tf_op jit(solution)/shard_map/to_core/ppermute | solution.py:338
  34.5 9.4 %collective-permute-start.6 = (f32[29,8,128]{2,1,0:T(8,128)S(1)}, f32[29,8,128]{2,1,0:T(8,128)S(1)}, u32[]{:S(2)}, u32[]{:S(2)}) collective-permute-start(f32[29,8,128]{2,1,0:T(8,128)S(1)} %get-tuple-element.58), channel_id=1, source_target_pairs={{0,2},{1,15},{2,4},{3,1},{4,6},{5,3},{6,8},{7,5},{8,10},{9,7},{10,... | collective-permute-start | bytes 356360 | tf_op jit(solution)/shard_map/from_owners/ppermute | solution.py:295
  35.6 14.8 %collective-permute-start.7 = (f32[29,8,128]{2,1,0:T(8,128)S(1)}, f32[29,8,128]{2,1,0:T(8,128)S(1)}, u32[]{:S(2)}, u32[]{:S(2)}) collective-permute-start(f32[29,8,128]{2,1,0:T(8,128)S(1)} %get-tuple-element.64), channel_id=1, source_target_pairs={{0,4},{1,13},{2,6},{3,15},{4,8},{5,1},{6,10},{7,3},{8,12},{9,5},{1... | collective-permute-start | bytes 356360 | tf_op jit(solution)/shard_map/from_owners/ppermute | solution.py:295
  38.4 12.0 %collective-permute-start.8 = (f32[29,8,128]{2,1,0:T(8,128)S(1)}, f32[29,8,128]{2,1,0:T(8,128)S(1)}, u32[]{:S(2)}, u32[]{:S(2)}) collective-permute-start(f32[29,8,128]{2,1,0:T(8,128)S(1)} %get-tuple-element.65), channel_id=1, source_target_pairs={{0,6},{1,11},{2,8},{3,13},{4,10},{5,15},{6,12},{7,1},{8,14},{9,3},... | collective-permute-start | bytes 356360 | tf_op jit(solution)/shard_map/from_owners/ppermute | solution.py:295
  39.4 11.0 %collective-permute-start.9 = (f32[15,8,128]{2,1,0:T(8,128)S(1)}, f32[15,8,128]{2,1,0:T(8,128)S(1)}, u32[]{:S(2)}, u32[]{:S(2)}) collective-permute-start(f32[15,8,128]{2,1,0:T(8,128)S(1)} %get-tuple-element.66), channel_id=1, source_target_pairs={{0,8},{1,9},{2,10},{3,11},{4,12},{5,13},{6,14},{7,15},{8,0},{9,1},... | collective-permute-start | bytes 184328 | tf_op jit(solution)/shard_map/from_owners/ppermute | solution.py:295
  50.5 1.8 %collective-permute-start.10 = (f32[102,8,128]{2,1,0:T(8,128)S(1)}, f32[102,8,128]{2,1,0:T(8,128)S(1)}, u32[]{:S(2)}, u32[]{:S(2)}) collective-permute-start(f32[102,8,128]{2,1,0:T(8,128)S(1)} %constant_dynamic-update-slice_fusion.6.refs_0_), channel_id=1, source_target_pairs={{0,1},{1,0},{2,3},{3,2},{4,5},{5,4},{6,7},{7,6},{8,9},{9,8},{10,11... | collective-permute-start | bytes 1253384 | tf_op jit(solution)/shard_map/states/ppermute | solution.py:365
  52.4 8.7 %collective-permute-start.11 = (f32[1,8,128]{2,1,0:T(8,128)S(1)}, f32[1,8,128]{2,1,0:T(8,128)S(1)}, u32[]{:S(2)}, u32[]{:S(2)}) collective-permute-start(f32[1,8,128]{2,1,0:T(8,128)S(1)} %slice_add_fusion), channel_id=1, source_target_pairs={{0,64},{64,128},{128,192},{192,0},{1,65},{65,129},{129,193},{193,1... | collective-permute-start | bytes 12296 | tf_op jit(solution)/shard_map/grad_gain/ppermute | solution.py:375
  54.0 7.0 %collective-permute-start.12 = (f32[1,8,128]{2,1,0:T(8,128)S(1)}, f32[1,8,128]{2,1,0:T(8,128)S(1)}, u32[]{:S(2)}, u32[]{:S(2)}) collective-permute-start(f32[1,8,128]{2,1,0:T(8,128)S(1)} %slice_add_fusion), channel_id=1, source_target_pairs={{0,128},{64,192},{128,0},{192,64},{1,129},{65,193},{129,1},{193,65... | collective-permute-start | bytes 12296 | tf_op jit(solution)/shard_map/grad_gain/ppermute | solution.py:375
  56.6 4.4 %collective-permute-start.13 = (f32[1,8,128]{2,1,0:T(8,128)S(1)}, f32[1,8,128]{2,1,0:T(8,128)S(1)}, u32[]{:S(2)}, u32[]{:S(2)}) collective-permute-start(f32[1,8,128]{2,1,0:T(8,128)S(1)} %slice_add_fusion), channel_id=1, source_target_pairs={{0,192},{64,0},{128,64},{192,128},{1,193},{65,1},{129,65},{193,129... | collective-permute-start | bytes 12296 | tf_op jit(solution)/shard_map/grad_gain/ppermute | solution.py:375

commit v2 on v1

--- a/solution.py
+++ b/solution.py
@@ -142,53 +142,72 @@
     own_ref[...] = give[chip].reshape(wide, UNIT, E)
 
 
-def intra_body(heads, factor, qs_ref, ks_ref, vs_ref, gy_ref, gain_ref, dq_ref, dk_ref, dv_ref, g_ref):
-    count = qs_ref.shape[0] // CHUNK
+def beside(*parts):
+    return jnp.concatenate(parts, axis=1)
+
+
+def over(*parts):
+    return jnp.concatenate(parts, axis=0)
+
+
+def intra_body(heads, factor, qs_ref, ks_ref, vs_ref, gy_ref, gain_ref, g_in, dq_ref, dk_ref, dv_ref, g_ref):
+    g_ref[...] = g_in[...]
     first = lax.broadcasted_iota(jnp.int32, (CHUNK, CHUNK), 0)
     second = lax.broadcasted_iota(jnp.int32, (CHUNK, CHUNK), 1)
     lower, upper = first >= second, first <= second
-
-    def twice(x, axis=1):
-        return jnp.concatenate([x, x], axis=axis)
-
-    def per_head(h, carry):
-        lanes = pl.ds(pl.multiple_of(h * E, E), E)
-        at = [slice(i * CHUNK, (i + 1) * CHUNK) for i in range(count)]
-        q, k, v, gy = ([ref[rows, lanes] for rows in at] for ref in (qs_ref, ks_ref, vs_ref, gy_ref))
-        gain = gain_ref[h]
-        g_hi, g_lo = halves(gain)
-        dq, dk, dv = [], [], []
+    zero = jnp.zeros((E, E), BF16)
+
+    for h in range(heads):
+        lanes = slice(h * E, (h + 1) * E)
+        at = [slice(i, i + CHUNK) for i in range(0, qs_ref.shape[0], CHUNK)]
+        q, k, v, gy = ([ref[some, lanes] for some in at] for ref in (qs_ref, ks_ref, vs_ref, gy_ref))
+        count = len(at)
+        gain = gain_ref[lanes].reshape(1, E)
+        down = jnp.transpose(jnp.broadcast_to(gain, (8, E)))[:, 0:1]
+        g_hi, g_lo = halves(down)
+        q_t, v_t, gy_t = ([x.T for x in y] for y in (q, v, gy))
+        both = [
+            mm(beside(v_t[i], gy_t[i]), over(beside(k[i], zero), beside(zero, q[i])), 1, 0)
+            for i in range(count)
+        ]
+        before, after = [None] * count, [None] * count
+        for i in range(1, count):
+            before[i] = both[i - 1][:, :E] if i == 1 else before[i - 1] + both[i - 1][:, :E]
+        for i in reversed(range(count - 1)):
+            after[i] = both[i + 1][:, E:] if i == count - 2 else after[i + 1] + both[i + 1][:, E:]
+        total = jnp.zeros((1, E), F32)
         for i in range(count):
-            vg = jnp.concatenate([v[i] * g_hi, v[i] * g_lo], axis=1)
-            weights = jnp.where(lower, mm(twice(gy[i]), vg, 1, 1), 0.0)
-            w_hi, w_lo = halves(weights)
-            dq.append(mm(jnp.concatenate([w_hi, w_lo], axis=1), twice(k[i], 0), 1, 0))
-            dk.append(mm(jnp.concatenate([w_hi, w_lo], axis=0), twice(q[i], 0), 0, 0))
-            s_hi, s_lo = halves(jnp.where(upper, mm(k[i], q[i], 1, 1), 0.0))
-            dv.append(mm(jnp.concatenate([s_hi, s_lo], axis=1), twice(gy[i], 0), 1, 0))
-        state = None
-        for i in range(count):
+            left = over(v_t[i] * g_hi, v_t[i] * g_lo)
             if i > 0:
-                kv = mm(k[i - 1], v[i - 1], 0, 0)
-                state = kv if state is None else state + kv
-                dq[i] += mm(twice(gy[i]), jnp.concatenate(halves(state * gain), axis=1), 1, 1)
-            dq_ref[at[i], lanes] = factor * dq[i]
-        state = None
-        total = jnp.zeros((1, E), F32)
-        for i in reversed(range(count)):
+                left = beside(left, over(*halves(before[i] * down)))
+            r = mm(beside(gy[i], gy[i]), left, 1, 0)
+            w = halves(jnp.where(lower, r[:, :E], 0.0))
+            dq = mm(beside(*w), over(k[i], k[i]), 1, 0)
+            if i > 0:
+                dq += r[:, E:]
+            dq_ref[at[i], lanes] = factor * dq
+            left = over(*halves(gy_t[i].astype(F32) * down))
             if i + 1 < count:
-                qd = mm(q[i + 1], gy[i + 1], 0, 0)
-                state = qd if state is None else state + qd
-                dk[i] += mm(twice(v[i]), jnp.concatenate(halves(state * gain), axis=1), 1, 1)
-                dv[i] += mm(twice(k[i]), jnp.concatenate(halves(state), axis=0), 1, 0)
-            dk_ref[at[i], lanes] = factor * dk[i]
-            dv_plain = factor * dv[i]
-            dv_ref[at[i], lanes] = dv_plain * gain
-            total = total + jnp.sum(v[i].astype(F32) * dv_plain, axis=0, keepdims=True)
-        g_ref[h] = total
-        return carry
-
-    lax.fori_loop(0, heads, per_head, 0)
+                left = beside(left, over(*halves(after[i] * down)))
+            r = mm(beside(v[i], v[i]), left, 1, 0)
+            w = halves(jnp.where(upper, r[:, :E], 0.0))
+            dk = mm(beside(*w), over(q[i], q[i]), 1, 0)
+            if i + 1 < count:
+                dk += r[:, E:]
+            dk_ref[at[i], lanes] = factor * dk
+            if i + 1 < count:
+                left = beside(over(q_t[i], zero), over(*halves(after[i].T)))
+                r = mm(beside(k[i], k[i]), left, 1, 0)
+            else:
+                r = mm(k[i], q_t[i], 1, 0)
+            s = halves(jnp.where(upper, r[:, :E], 0.0))
+            dv = mm(beside(*s), over(gy[i], gy[i]), 1, 0)
+            if i + 1 < count:
+                dv += r[:, E:]
+            dv = factor * dv
+            dv_ref[at[i], lanes] = dv * gain
+            total = total + jnp.sum(v[i].astype(F32) * dv, axis=0, keepdims=True)
+        g_ref[0, h : h + 1] += total
 
 
 def slope_body(q_ref, k_ref, v_ref, sq_ref, sk_ref, sv_ref):
@@ -235,7 +254,7 @@
     copies = []
     for h in range(heads):
         lanes = slice(h * E, (h + 1) * E)
-        gain = gain_ref[h]
+        gain = gain_ref[lanes].reshape(1, E)
         gy, k, v = gy_ref[:, lanes], ks_ref[:, lanes], vs_ref[:, lanes]
         m2 = jnp.concatenate(halves(state[0, h] * (gain * factor)), axis=1)
         g_hi, g_lo = halves(state[1, h] * gain)
@@ -257,6 +276,25 @@
         copy.wait()
 
 
+def pack_body(*refs):
+    *parts, out_ref = refs
+    base = 0
+    for ref in parts:
+        out_ref[base : base + ref.shape[0]] = ref[...]
+        base += ref.shape[0]
+
+
+def collect_body(*refs):
+    *parts, g_ref, out_ref = refs
+    pack_body(*parts, out_ref)
+    core = lax.rem(lax.axis_index("ctx"), 2)
+    far = g_ref[...] + parts[-1][parts[-1].shape[0] - 1 :]
+    total = jnp.where(core == 0, far, 0.0)
+    for ref in parts[:-1]:
+        total = total + ref[ref.shape[0] - 1 :]
+    out_ref[out_ref.shape[0] - 1 :] = total
+
+
 def params(mib, **more):
     return pltpu.CompilerParams(vmem_limit_bytes=mib * 1024 * 1024, **more)
 
@@ -274,7 +312,6 @@
     factor = 1.0 / math.sqrt(E * rows * devices)
     units = E // UNIT
     assert units == devices and near == 4
-    gain_h = gain.reshape(heads, 1, E)
 
     def shape(*dims, dtype=F32):
         return jax.ShapeDtypeStruct(dims, dtype)
@@ -323,18 +360,22 @@
         parts = exchange(parts)
 
     with jax.named_scope("intra"):
-        gain_late, parts[0] = lax.optimization_barrier((gain_h, parts[0]))
-        dq, dk, dv, g_intra = pl.pallas_call(
+        gain_late, parts[0] = lax.optimization_barrier((gain, parts[0]))
+        dq, dk, dv, g_mine = pl.pallas_call(
             lambda *refs: intra_body(heads, factor, *refs),
-            out_shape=[shape(rows, width)] * 3 + [shape(heads, 1, E)],
+            out_shape=[shape(rows, width)] * 3 + [tiles(1)],
             compiler_params=params(4),
             cost_estimate=cost(7),
             name="intra",
-        )(q_spike, k_spike, v_spike, gy, gain_late)
+        )(q_spike, k_spike, v_spike, gy, gain_late, g_chip)
 
     with jax.named_scope("to_core"):
-        g_mine = g_chip + jnp.pad(g_intra.reshape(1, heads, E), ((0, 0), (0, UNIT - heads), (0, 0)))
-        pack = jnp.concatenate([*parts, own, g_mine])
+        pack = pl.pallas_call(
+            pack_body,
+            out_shape=tiles(4 * heads * near + 1),
+            compiler_params=params(2),
+            name="pack",
+        )(*parts, own, g_mine)
         pack_got = lax.ppermute(pack, "ctx", swap)
 
     with jax.named_scope("scan"):
@@ -361,14 +402,16 @@
 
     with jax.named_scope("states"):
         sq, *parts = lax.optimization_barrier((sq, *parts))
-        mine = jnp.concatenate(parts)
+        mine = pl.pallas_call(
+            collect_body,
+            out_shape=tiles((4 * heads + 1) * near - 2 * heads),
+            compiler_params=params(2),
+            name="collect",
+        )(*parts, g_all)
         theirs = lax.ppermute(mine, "ctx", swap)
 
     with jax.named_scope("grad_gain"):
-        lasts = [(4 * heads + 1) * (i + 1) - 1 for i in range(near - 1)]
-        g_sum = g_all + mine[-1:]
-        for i in lasts:
-            g_sum = g_sum + mine[i : i + 1] + theirs[i : i + 1]
+        g_sum = mine[-1:] + theirs[-1:]
         size = lax.axis_size("dp")
         total = g_sum
         for step in range(1, size):
@@ -391,7 +434,7 @@
             ],
             compiler_params=params(8),
             name="finish",
-        )(mine, theirs, own, got, gain_h, gy, k_spike, v_spike, dq, dk, dv, sq, sk, sv)
+        )(mine, theirs, own, got, gain, gy, k_spike, v_spike, dq, dk, dv, sq, sk, sv)
     return (*grads, grad_gain)
 
 

time: 62.1 us -> 57.3 us (0.923)
  waiting for transfers between devices: 7.95 us -> 16.4 us
  Pallas kernels: 22.1 us -> 16.6 us
  starting transfers between devices: 27.1 us -> 22.8 us
  local copies, waits for them, and re-layouts: 3.61 us -> 0.62 us
    ppermute x8, waiting for transfers between devices: 2.61 us -> 9.71 us  [exchange(): lax.ppermute(part, 'ctx', ring(k))]
    pallas_call x1, Pallas kernels: 10.5 us -> 5.64 us  [per_device(): pl.pallas_call(lambda *refs: intra_body(heads, factor, *refs), out_shape=...]
    unnamed x26 -> x8, local copies, waits for them, and re-layouts: 3 us -> 0.02 us
    ppermute x1, starting transfers between devices: 2.14 us -> 0.09 us  [per_device(): pack_got = lax.ppermute(pack, 'ctx', swap)]
    ppermute x3, starting transfers between devices: 5.67 us -> 4.45 us  [per_device(): lax.ppermute(g_sum, 'dp', [(i, (i + step) % size) for i in range(size)])]
    ppermute x8, starting transfers between devices: 19.1 us -> 18.1 us  [exchange(): lax.ppermute(part, 'ctx', ring(k))]
    ppermute x3, waiting for transfers between devices: 0.01 us -> 1.04 us  [per_device(): lax.ppermute(g_sum, 'dp', [(i, (i + step) % size) for i in range(size)])]
  transfers between devices with their start and end apart: 14 -> 14, of which waited for: 4 -> 7; matrix products, arithmetic and copies ran while one was open for 2% -> 0% of each run, Pallas kernels for 28% -> 22%
where the time goes in v2:
time: 57.3 us; the launch traced here: 57.2 us
  starting transfers between devices  22.8 us (40%)
  Pallas kernels  16.6 us (29%)
  waiting for transfers between devices  16.4 us (29%)
  between operations  0.78 us (1%)
  local copies, waits for them, and re-layouts  0.62 us (1%)
    ppermute x8, starting transfers between devices, exchange(): lax.ppermute(part, 'ctx', ring(k))  18.1 us
    ppermute x8, waiting for transfers between devices, exchange(): lax.ppermute(part, 'ctx', ring(k))  9.71 us
    pallas_call x1, Pallas kernels, per_device(): pl.pallas_call(lambda *refs: intra_body(heads, factor, *refs), out_shape=...  5.64 us
    ppermute x3, starting transfers between devices, per_device(): lax.ppermute(g_sum, 'dp', [(i, (i + step) % size) for i in range(size)])  4.45 us
    pallas_call x1, Pallas kernels, per_device(): pl.pallas_call(slope_body, out_shape=[shape(rows, width)] * 3, compiler_p...  3.92 us
    pallas_call x1, Pallas kernels, per_device(): pl.pallas_call(lambda *refs: states_body(chips, heads, factor, *refs), in...  3.79 us
    pallas_call x1, Pallas kernels, per_device(): pl.pallas_call(lambda *refs: finish_body(chips, heads, factor, *refs), in...  2.9 us
    ppermute x1, waiting for transfers between devices, per_device(): got = lax.ppermute(send, 'ctx', swap)  2.13 us
  transfers between devices with their start and end apart: 14, of which 7 were waited for; matrix products, arithmetic and copies ran while one was open for 0% of the time, Pallas kernels for 22%

profile of v2, /device:TPU:16, one launch (start us, length us, event | category | flops | bytes accessed | tf_op | source)
XLA Modules:
  0.0 57.2 jit_solution(8393623431614928850)
XLA Ops:
  0.6 0.0 copy-start
  0.6 3.8 %local_states.1 = (f32[16,7,8,128]{3,2,1,0:T(8,128)S(1)}, f32[24,7,8,128]{3,2,1,0:T(8,128)S(1)}, bf16[512,896]{1,0:T(8,128)(2,1)S(1)}, bf16[512,896]{1,0:T(8,128...) custom-call(s32[1,512,896]{2,1,0:T(8,128)} %refs_0_.1, s32[1,512,896]{2,1,0:T(8,128)} %refs_1_.1, ...), custom_call_target="tpu_custom_call" | custom-call | flops 3000000000 | bytes 6000000 | tf_op jit(solution)/shard_map/local_states/local_states/pallas_call | solution.py:335
  4.4 0.1 collective-permute-start
  4.5 2.1 %collective-permute-done.refs_1_.refs_3_ = f32[24,7,8,128]{3,2,1,0:T(8,128)S(1)} collective-permute-done((f32[24,7,8,128]{3,2,1,0:T(8,128)S(1)}, f32[24,7,8,128]{3,2,1,0:T(8,128)S(1)}, u32[]{:S(2)}, u32[]{:S(2)}) %collective-permute-start) | collective-permute-done | bytes 688160 | tf_op jit(solution)/shard_map/local_states/ppermute | solution.py:349
  6.7 0.1 chip_states.1
  6.8 2.0 %collective-permute-start.1 = (f32[28,8,128]{2,1,0:T(8,128)S(1)}, f32[28,8,128]{2,1,0:T(8,128)S(1)}, u32[]{:S(2)}, u32[]{:S(2)}) collective-permute-start(f32[28,8,128]{2,1,0:T(8,128)S(1)} %get-tuple-element.45), channel_id=1, source_target_pairs={{0,2},{1,15},{2,4},{3,1},{4,6},{5,3},{6,8},{7,5},{8,10},{9,7},{10,... | collective-permute-start | bytes 344072 | tf_op jit(solution)/shard_map/to_owners/ppermute | solution.py:332
  8.7 6.3 %collective-permute-start.4 = (f32[14,8,128]{2,1,0:T(8,128)S(1)}, f32[14,8,128]{2,1,0:T(8,128)S(1)}, u32[]{:S(2)}, u32[]{:S(2)}) collective-permute-start(f32[14,8,128]{2,1,0:T(8,128)S(1)} %get-tuple-element.49), channel_id=1, source_target_pairs={{0,8},{1,9},{2,10},{3,11},{4,12},{5,13},{6,14},{7,15},{8,0},{9,1},... | collective-permute-start | bytes 172040 | tf_op jit(solution)/shard_map/to_owners/ppermute | solution.py:332
  15.0 1.5 %collective-permute-start.2 = (f32[28,8,128]{2,1,0:T(8,128)S(1)}, f32[28,8,128]{2,1,0:T(8,128)S(1)}, u32[]{:S(2)}, u32[]{:S(2)}) collective-permute-start(f32[28,8,128]{2,1,0:T(8,128)S(1)} %get-tuple-element.47), channel_id=1, source_target_pairs={{0,4},{1,13},{2,6},{3,15},{4,8},{5,1},{6,10},{7,3},{8,12},{9,5},{1... | collective-permute-start | bytes 344072 | tf_op jit(solution)/shard_map/to_owners/ppermute | solution.py:332
  16.5 0.1 collective-permute-start.3
  16.6 0.0 collective-permute-done.1.refs_0_
  16.6 0.0 copy-done
  16.6 0.0 copy-start.3
  16.6 5.6 %intra.1 = (f32[512,896]{1,0:T(8,128)S(1)}, f32[512,896]{1,0:T(8,128)S(1)}, f32[512,896]{1,0:T(8,128)S(1)}, f32[1,8,128]{2,1,0:T(8,128)S(1)}) custom-call(bf16[512,896]{1,0:T(8,128)(2,1)S(1)} %get-tuple-element.51.refs_0_, bf16[512,896]{1,0:T(8,128)(2,1)S(1)} %get-tuple-element.52.refs_1_.refs_6_, bf16[512,896]{1,0:T(8,128)(2,1)S(1)} %get-tuple-element.53.refs_2_.refs_7_, ...), custom_call_target="tpu_custom_call" | custom-call | flops 7000000000 | bytes 14000000 | tf_op jit(solution)/shard_map/intra/intra/pallas_call | solution.py:364
  22.2 0.0 copy-start.1
  22.3 0.0 copy-start.2
  22.3 0.0 collective-permute-done.4.refs_3_
  22.3 0.0 collective-permute-done.2.refs_1_
  22.3 4.9 %collective-permute-done.3.refs_2_ = f32[28,8,128]{2,1,0:T(8,128)S(1)} collective-permute-done((f32[28,8,128]{2,1,0:T(8,128)S(1)}, f32[28,8,128]{2,1,0:T(8,128)S(1)}, u32[]{:S(2)}, u32[]{:S(2)}) %collective-permute-start.3) | collective-permute-done | bytes 114720 | tf_op jit(solution)/shard_map/to_owners/ppermute | solution.py:332
  27.2 0.1 collective-permute-start.5
  27.3 1.8 %collective-permute-done.5.refs_1_ = f32[113,8,128]{2,1,0:T(8,128)S(1)} collective-permute-done((f32[113,8,128]{2,1,0:T(8,128)S(1)}, f32[113,8,128]{2,1,0:T(8,128)S(1)}, u32[]{:S(2)}, u32[]{:S(2)}) %collective-permute-start.5) | collective-permute-done | bytes 462880 | tf_op jit(solution)/shard_map/to_core/ppermute | solution.py:379
  29.1 0.2 scan.1
  29.3 0.8 %collective-permute-start.6 = (f32[29,8,128]{2,1,0:T(8,128)S(1)}, f32[29,8,128]{2,1,0:T(8,128)S(1)}, u32[]{:S(2)}, u32[]{:S(2)}) collective-permute-start(f32[29,8,128]{2,1,0:T(8,128)S(1)} %get-tuple-element.58), channel_id=1, source_target_pairs={{0,2},{1,15},{2,4},{3,1},{4,6},{5,3},{6,8},{7,5},{8,10},{9,7},{10,... | collective-permute-start | bytes 356360 | tf_op jit(solution)/shard_map/from_owners/ppermute | solution.py:332
  30.1 3.7 %collective-permute-start.9 = (f32[15,8,128]{2,1,0:T(8,128)S(1)}, f32[15,8,128]{2,1,0:T(8,128)S(1)}, u32[]{:S(2)}, u32[]{:S(2)}) collective-permute-start(f32[15,8,128]{2,1,0:T(8,128)S(1)} %get-tuple-element.66), channel_id=1, source_target_pairs={{0,8},{1,9},{2,10},{3,11},{4,12},{5,13},{6,14},{7,15},{8,0},{9,1},... | collective-permute-start | bytes 184328 | tf_op jit(solution)/shard_map/from_owners/ppermute | solution.py:332
  33.7 0.6 %collective-permute-start.7 = (f32[29,8,128]{2,1,0:T(8,128)S(1)}, f32[29,8,128]{2,1,0:T(8,128)S(1)}, u32[]{:S(2)}, u32[]{:S(2)}) collective-permute-start(f32[29,8,128]{2,1,0:T(8,128)S(1)} %get-tuple-element.64), channel_id=1, source_target_pairs={{0,4},{1,13},{2,6},{3,15},{4,8},{5,1},{6,10},{7,3},{8,12},{9,5},{1... | collective-permute-start | bytes 356360 | tf_op jit(solution)/shard_map/from_owners/ppermute | solution.py:332
  34.3 3.2 %collective-permute-start.8 = (f32[29,8,128]{2,1,0:T(8,128)S(1)}, f32[29,8,128]{2,1,0:T(8,128)S(1)}, u32[]{:S(2)}, u32[]{:S(2)}) collective-permute-start(f32[29,8,128]{2,1,0:T(8,128)S(1)} %get-tuple-element.65), channel_id=1, source_target_pairs={{0,6},{1,11},{2,8},{3,13},{4,10},{5,15},{6,12},{7,1},{8,14},{9,3},... | collective-permute-start | bytes 356360 | tf_op jit(solution)/shard_map/from_owners/ppermute | solution.py:332
  37.5 0.0 collective-permute-done.6.refs_0_
  37.5 0.0 copy-done.3
  37.5 0.0 copy-done.1
  37.5 0.0 copy-done.2
  37.5 3.9 %slopes.1 = (f32[512,896]{1,0:T(8,128)S(1)}, f32[512,896]{1,0:T(8,128)S(1)}, f32[512,896]{1,0:T(8,128)S(1)}) custom-call(bf16[1,512,896]{2,1,0:T(8,128)(2,1)S(1)} %copy-done.1, bf16[1,512,896]{2,1,0:T(8,128)(2,1)S(1)} %copy-done.2, bf16[1,512,896]{2,1,0:T(8,128)(2,1)S(1)} %copy-done.3), custom_call_target="tpu_custom_call" | custom-call | flops 5000000000 | bytes 10000000 | tf_op jit(solution)/shard_map/slopes/slopes/pallas_call | solution.py:395
  41.5 0.0 collective-permute-done.9.refs_3_
  41.5 0.0 collective-permute-done.7.refs_1_
  41.5 4.8 %collective-permute-done.8.refs_2_ = f32[29,8,128]{2,1,0:T(8,128)S(1)} collective-permute-done((f32[29,8,128]{2,1,0:T(8,128)S(1)}, f32[29,8,128]{2,1,0:T(8,128)S(1)}, u32[]{:S(2)}, u32[]{:S(2)}) %collective-permute-start.8) | collective-permute-done | bytes 118816 | tf_op jit(solution)/shard_map/from_owners/ppermute | solution.py:332
  46.4 0.1 collective-permute-start.10
  46.5 1.7 %collective-permute-done.10.refs_1_ = f32[102,8,128]{2,1,0:T(8,128)S(1)} collective-permute-done((f32[102,8,128]{2,1,0:T(8,128)S(1)}, f32[102,8,128]{2,1,0:T(8,128)S(1)}, u32[]{:S(2)}, u32[]{:S(2)}) %collective-permute-start.10) | collective-permute-done | bytes 417824 | tf_op jit(solution)/shard_map/states/ppermute | solution.py:411
  48.2 2.8 %collective-permute-start.13 = (f32[1,8,128]{2,1,0:T(8,128)S(1)}, f32[1,8,128]{2,1,0:T(8,128)S(1)}, u32[]{:S(2)}, u32[]{:S(2)}) collective-permute-start(f32[1,8,128]{2,1,0:T(8,128)S(1)} %slice_add_fusion), channel_id=1, source_target_pairs={{0,192},{64,0},{128,64},{192,128},{1,193},{65,1},{129,65},{193,129... | collective-permute-start | bytes 12296 | tf_op jit(solution)/shard_map/grad_gain/ppermute | solution.py:418
  51.0 0.8 %collective-permute-start.12 = (f32[1,8,128]{2,1,0:T(8,128)S(1)}, f32[1,8,128]{2,1,0:T(8,128)S(1)}, u32[]{:S(2)}, u32[]{:S(2)}) collective-permute-start(f32[1,8,128]{2,1,0:T(8,128)S(1)} %slice_add_fusion), channel_id=1, source_target_pairs={{0,128},{64,192},{128,0},{192,64},{1,129},{65,193},{129,1},{193,65... | collective-permute-start | bytes 12296 | tf_op jit(solution)/shard_map/grad_gain/ppermute | solution.py:418
  51.8 0.9 %collective-permute-start.11 = (f32[1,8,128]{2,1,0:T(8,128)S(1)}, f32[1,8,128]{2,1,0:T(8,128)S(1)}, u32[]{:S(2)}, u32[]{:S(2)}) collective-permute-start(f32[1,8,128]{2,1,0:T(8,128)S(1)} %slice_add_fusion), channel_id=1, source_target_pairs={{0,64},{64,128},{128,192},{192,0},{1,65},{65,129},{129,193},{193,1... | collective-permute-start | bytes 12296 | tf_op jit(solution)/shard_map/grad_gain/ppermute | solution.py:418
  52.7 2.9 %finish.1 = (bf16[1,512,896]{2,1,0:T(8,128)(2,1)}, bf16[1,512,896]{2,1,0:T(8,128)(2,1)}, bf16[1,512,896]{2,1,0:T(8,128)(2,1)}) custom-call(f32[102,8,128]{2,1,0:T(8,128)S(1)} %collect.1.refs_0_, f32[102,8,128]{2,1,0:T(8,128)S(1)} %collective-permute-done.10.refs_1_, f32[28,8,128]{2,1,0:T(8,128)S(1)} %get-tuple-element.72.refs_2_, ...), custom_call_target="tpu_custom_call" | custom-call | tf_op jit(solution)/shard_map/finish/finish/pallas_call | solution.py:425
  55.6 0.0 collective-permute-done.13
  55.6 0.5 collective-permute-done.12
  56.1 0.5 collective-permute-done.11
  56.6 0.6 %slice_bitcast_fusion = f32[896]{0:T(1024)} fusion(f32[1,8,128]{2,1,0:T(8,128)S(1)} %add_add_fusion), kind=kLoop, calls=%fused_computation.1 | loop fusion | bytes 7168 | tf_op jit(solution)/shard_map/grad_gain/reshape;grad_gain/squeeze | solution.py:421
  (4 shorter events, 0.1 us)
Async XLA Ops:
  0.6 16.0 %copy-start = (f32[896]{0:T(1024)S(1)}, f32[896]{0:T(1024)}, u32[]{:S(2)}) copy-start(f32[896]{0:T(1024)} %refs_4_.2) | copy-start | bytes 10756
  4.4 2.2 %collective-permute-start = (f32[24,7,8,128]{3,2,1,0:T(8,128)S(1)}, f32[24,7,8,128]{3,2,1,0:T(8,128)S(1)}, u32[]{:S(2)}, u32[]{:S(2)}) collective-permute-start(f32[24,7,8,128]{3,2,1,0:T(8,128)S(1)} %get-tuple-element.44), channel_id=1, source_target_pairs={{0,1},{1,0},{2,3},{3,2},{4,5},{5,4},{6,7},{7,6},{8,9},{9,8},{10,11... | collective-permute-start | bytes 2064392 | tf_op jit(solution)/shard_map/local_states/ppermute | solution.py:349
  6.8 9.8 %collective-permute-start.1 = (f32[28,8,128]{2,1,0:T(8,128)S(1)}, f32[28,8,128]{2,1,0:T(8,128)S(1)}, u32[]{:S(2)}, u32[]{:S(2)}) collective-permute-start(f32[28,8,128]{2,1,0:T(8,128)S(1)} %get-tuple-element.45), channel_id=1, source_target_pairs={{0,2},{1,15},{2,4},{3,1},{4,6},{5,3},{6,8},{7,5},{8,10},{9,7},{10,... | collective-permute-start | bytes 344072 | tf_op jit(solution)/shard_map/to_owners/ppermute | solution.py:332
  8.7 13.5 %collective-permute-start.4 = (f32[14,8,128]{2,1,0:T(8,128)S(1)}, f32[14,8,128]{2,1,0:T(8,128)S(1)}, u32[]{:S(2)}, u32[]{:S(2)}) collective-permute-start(f32[14,8,128]{2,1,0:T(8,128)S(1)} %get-tuple-element.49), channel_id=1, source_target_pairs={{0,8},{1,9},{2,10},{3,11},{4,12},{5,13},{6,14},{7,15},{8,0},{9,1},... | collective-permute-start | bytes 172040 | tf_op jit(solution)/shard_map/to_owners/ppermute | solution.py:332
  15.0 7.2 %collective-permute-start.2 = (f32[28,8,128]{2,1,0:T(8,128)S(1)}, f32[28,8,128]{2,1,0:T(8,128)S(1)}, u32[]{:S(2)}, u32[]{:S(2)}) collective-permute-start(f32[28,8,128]{2,1,0:T(8,128)S(1)} %get-tuple-element.47), channel_id=1, source_target_pairs={{0,4},{1,13},{2,6},{3,15},{4,8},{5,1},{6,10},{7,3},{8,12},{9,5},{1... | collective-permute-start | bytes 344072 | tf_op jit(solution)/shard_map/to_owners/ppermute | solution.py:332
  16.5 10.7 %collective-permute-start.3 = (f32[28,8,128]{2,1,0:T(8,128)S(1)}, f32[28,8,128]{2,1,0:T(8,128)S(1)}, u32[]{:S(2)}, u32[]{:S(2)}) collective-permute-start(f32[28,8,128]{2,1,0:T(8,128)S(1)} %get-tuple-element.48), channel_id=1, source_target_pairs={{0,6},{1,11},{2,8},{3,13},{4,10},{5,15},{6,12},{7,1},{8,14},{9,3},... | collective-permute-start | bytes 344072 | tf_op jit(solution)/shard_map/to_owners/ppermute | solution.py:332
  16.6 20.9 %copy-start.3 = (bf16[1,512,896]{2,1,0:T(8,128)(2,1)S(1)}, bf16[1,512,896]{2,1,0:T(8,128)(2,1)}, u32[]{:S(2)}) copy-start(bf16[1,512,896]{2,1,0:T(8,128)(2,1)} %v_ref) | copy-start | bytes 2752516
  22.2 15.3 %copy-start.1 = (bf16[1,512,896]{2,1,0:T(8,128)(2,1)S(1)}, bf16[1,512,896]{2,1,0:T(8,128)(2,1)}, u32[]{:S(2)}) copy-start(bf16[1,512,896]{2,1,0:T(8,128)(2,1)} %q_ref) | copy-start | bytes 2752516
  22.3 15.3 %copy-start.2 = (bf16[1,512,896]{2,1,0:T(8,128)(2,1)S(1)}, bf16[1,512,896]{2,1,0:T(8,128)(2,1)}, u32[]{:S(2)}) copy-start(bf16[1,512,896]{2,1,0:T(8,128)(2,1)} %k_ref) | copy-start | bytes 2752516
  27.2 1.9 %collective-permute-start.5 = (f32[113,8,128]{2,1,0:T(8,128)S(1)}, f32[113,8,128]{2,1,0:T(8,128)S(1)}, u32[]{:S(2)}, u32[]{:S(2)}) collective-permute-start(f32[113,8,128]{2,1,0:T(8,128)S(1)} %pack.1.refs_0_), channel_id=1, source_target_pairs={{0,1},{1,0},{2,3},{3,2},{4,5},{5,4},{6,7},{7,6},{8,9},{9,8},{10,11... | collective-permute-start | bytes 1388552 | tf_op jit(solution)/shard_map/to_core/ppermute | solution.py:379
  29.3 8.2 %collective-permute-start.6 = (f32[29,8,128]{2,1,0:T(8,128)S(1)}, f32[29,8,128]{2,1,0:T(8,128)S(1)}, u32[]{:S(2)}, u32[]{:S(2)}) collective-permute-start(f32[29,8,128]{2,1,0:T(8,128)S(1)} %get-tuple-element.58), channel_id=1, source_target_pairs={{0,2},{1,15},{2,4},{3,1},{4,6},{5,3},{6,8},{7,5},{8,10},{9,7},{10,... | collective-permute-start | bytes 356360 | tf_op jit(solution)/shard_map/from_owners/ppermute | solution.py:332
  30.1 11.4 %collective-permute-start.9 = (f32[15,8,128]{2,1,0:T(8,128)S(1)}, f32[15,8,128]{2,1,0:T(8,128)S(1)}, u32[]{:S(2)}, u32[]{:S(2)}) collective-permute-start(f32[15,8,128]{2,1,0:T(8,128)S(1)} %get-tuple-element.66), channel_id=1, source_target_pairs={{0,8},{1,9},{2,10},{3,11},{4,12},{5,13},{6,14},{7,15},{8,0},{9,1},... | collective-permute-start | bytes 184328 | tf_op jit(solution)/shard_map/from_owners/ppermute | solution.py:332
  33.7 7.8 %collective-permute-start.7 = (f32[29,8,128]{2,1,0:T(8,128)S(1)}, f32[29,8,128]{2,1,0:T(8,128)S(1)}, u32[]{:S(2)}, u32[]{:S(2)}) collective-permute-start(f32[29,8,128]{2,1,0:T(8,128)S(1)} %get-tuple-element.64), channel_id=1, source_target_pairs={{0,4},{1,13},{2,6},{3,15},{4,8},{5,1},{6,10},{7,3},{8,12},{9,5},{1... | collective-permute-start | bytes 356360 | tf_op jit(solution)/shard_map/from_owners/ppermute | solution.py:332
  34.3 12.0 %collective-permute-start.8 = (f32[29,8,128]{2,1,0:T(8,128)S(1)}, f32[29,8,128]{2,1,0:T(8,128)S(1)}, u32[]{:S(2)}, u32[]{:S(2)}) collective-permute-start(f32[29,8,128]{2,1,0:T(8,128)S(1)} %get-tuple-element.65), channel_id=1, source_target_pairs={{0,6},{1,11},{2,8},{3,13},{4,10},{5,15},{6,12},{7,1},{8,14},{9,3},... | collective-permute-start | bytes 356360 | tf_op jit(solution)/shard_map/from_owners/ppermute | solution.py:332
  46.4 1.8 %collective-permute-start.10 = (f32[102,8,128]{2,1,0:T(8,128)S(1)}, f32[102,8,128]{2,1,0:T(8,128)S(1)}, u32[]{:S(2)}, u32[]{:S(2)}) collective-permute-start(f32[102,8,128]{2,1,0:T(8,128)S(1)} %collect.1.refs_0_), channel_id=1, source_target_pairs={{0,1},{1,0},{2,3},{3,2},{4,5},{5,4},{6,7},{7,6},{8,9},{9,8},{10,11... | collective-permute-start | bytes 1253384 | tf_op jit(solution)/shard_map/states/ppermute | solution.py:411
  48.2 7.4 %collective-permute-start.13 = (f32[1,8,128]{2,1,0:T(8,128)S(1)}, f32[1,8,128]{2,1,0:T(8,128)S(1)}, u32[]{:S(2)}, u32[]{:S(2)}) collective-permute-start(f32[1,8,128]{2,1,0:T(8,128)S(1)} %slice_add_fusion), channel_id=1, source_target_pairs={{0,192},{64,0},{128,64},{192,128},{1,193},{65,1},{129,65},{193,129... | collective-permute-start | bytes 12296 | tf_op jit(solution)/shard_map/grad_gain/ppermute | solution.py:418
  51.0 5.1 %collective-permute-start.12 = (f32[1,8,128]{2,1,0:T(8,128)S(1)}, f32[1,8,128]{2,1,0:T(8,128)S(1)}, u32[]{:S(2)}, u32[]{:S(2)}) collective-permute-start(f32[1,8,128]{2,1,0:T(8,128)S(1)} %slice_add_fusion), channel_id=1, source_target_pairs={{0,128},{64,192},{128,0},{192,64},{1,129},{65,193},{129,1},{193,65... | collective-permute-start | bytes 12296 | tf_op jit(solution)/shard_map/grad_gain/ppermute | solution.py:418
  51.8 4.8 %collective-permute-start.11 = (f32[1,8,128]{2,1,0:T(8,128)S(1)}, f32[1,8,128]{2,1,0:T(8,128)S(1)}, u32[]{:S(2)}, u32[]{:S(2)}) collective-permute-start(f32[1,8,128]{2,1,0:T(8,128)S(1)} %slice_add_fusion), channel_id=1, source_target_pairs={{0,64},{64,128},{128,192},{192,0},{1,65},{65,129},{129,193},{193,1... | collective-permute-start | bytes 12296 | tf_op jit(solution)/shard_map/grad_gain/ppermute | solution.py:418

commit v3 on v2

--- a/solution.py
+++ b/solution.py
@@ -67,7 +67,7 @@
 
 def states_body(
     chips, heads, factor, q_ref, k_ref, v_ref, gy_ref,
-    keep_ref, send_ref, qs_ref, ks_ref, vs_ref, gy_out, counts, both, sems,
+    keep_ref, send_ref, side_ref, qs_ref, ks_ref, vs_ref, gy_out, counts, both, sems,
 ):
     chip, core, way = place()
     mine = unit_list(chip, core, way, chips)
@@ -94,7 +94,7 @@
         for t in range(2):
             keep_ref[2 * i + t] = both[t, :, rows_of(here)]
             send_ref[2 * i + t] = both[t, :, rows_of(there)]
-        send_ref[2 * len(mine) + i] = both[core, :, rows_of(here)]
+        side_ref[i] = both[core, :, rows_of(here)]
 
 
 def chip_body(chips, heads, keep_ref, got_ref, m1_ref, m2_ref, m3_ref, m4_ref, own_ref, g_ref):
@@ -223,24 +223,25 @@
 
 
 def finish_body(
-    chips, heads, factor, u_ref, w_ref, own_ref, got_ref, gain_ref, gy_ref, ks_ref, vs_ref,
+    chips, heads, factor, u1_ref, u2_ref, w1_ref, w2_ref, own_ref, got_ref, side_ref, gain_ref, gy_ref, ks_ref, vs_ref,
     dq_ref, dk_ref, dv_ref, sq_ref, sk_ref, sv_ref, oq_ref, ok_ref, ov_ref,
     state, stage, sems,
 ):
     chip, core, way = place()
     wide, near = 4 * heads, chips // 2
     tiles = wide + 1
-    for ref, go, lane in ((u_ref, way, core), (w_ref, -way, 1 - core)):
-        for k in range(1, near):
+    both = ((u1_ref, u2_ref, way, core), (w1_ref, w2_ref, -way, 1 - core))
+    for one_ref, two_ref, go, lane in both:
+        for k, ref, start in ((1, one_ref, 0), (2, one_ref, tiles), (3, two_ref, 0)):
             shard = around(chip, -go * k, chips)
             for b in range(2):
                 for t in range(2):
-                    base = tiles * (k - 1) + (2 * b + t) * heads
+                    base = start + (2 * b + t) * heads
                     state[t, :, rows_of(2 * shard + b)] = ref[base : base + heads]
         for t in range(2):
-            base = tiles * (near - 1) + t * heads
+            base = tiles + t * heads
             unit = 2 * around(chip, near, chips) + lane
-            state[t, :, rows_of(unit)] = ref[base : base + heads]
+            state[t, :, rows_of(unit)] = two_ref[base : base + heads]
     for b in range(2):
         for t in range(2):
             base = (2 * b + t) * heads
@@ -250,7 +251,7 @@
     other = unit_list(chip, 1 - core, -way, chips)
     for i, (here, there) in enumerate(zip(mine, other)):
         state[kind, :, rows_of(here)] += got_ref[2 * i + kind]
-        state[kind, :, rows_of(there)] += got_ref[2 * len(mine) + i]
+        state[kind, :, rows_of(there)] += side_ref[i]
     copies = []
     for h in range(heads):
         lanes = slice(h * E, (h + 1) * E)
@@ -284,15 +285,13 @@
         base += ref.shape[0]
 
 
-def collect_body(*refs):
-    *parts, g_ref, out_ref = refs
-    pack_body(*parts, out_ref)
+def collect_body(first_ref, third_ref, fourth_ref, g_ref, out_ref):
+    pack_body(third_ref, fourth_ref, out_ref)
     core = lax.rem(lax.axis_index("ctx"), 2)
-    far = g_ref[...] + parts[-1][parts[-1].shape[0] - 1 :]
-    total = jnp.where(core == 0, far, 0.0)
-    for ref in parts[:-1]:
-        total = total + ref[ref.shape[0] - 1 :]
-    out_ref[out_ref.shape[0] - 1 :] = total
+    tiles, last = third_ref.shape[0], out_ref.shape[0] - 1
+    total = jnp.where(core == 0, g_ref[...] + fourth_ref[last - tiles :], 0.0)
+    total = total + first_ref[tiles - 1 : tiles] + first_ref[2 * tiles - 1 :]
+    out_ref[last:] = total + third_ref[tiles - 1 :]
 
 
 def params(mib, **more):
@@ -332,10 +331,11 @@
         return [lax.ppermute(part, "ctx", ring(k)) for k, part in enumerate(parts, 1)]
 
     with jax.named_scope("local_states"):
-        keep, send, q_spike, k_spike, v_spike, gy = pl.pallas_call(
+        keep, send, side, q_spike, k_spike, v_spike, gy = pl.pallas_call(
             lambda *refs: states_body(chips, heads, factor, *refs),
             in_specs=[pl.BlockSpec(memory_space=pltpu.HBM)] * 4,
-            out_shape=[shape(units, heads, UNIT, E), shape(units * 3 // 2, heads, UNIT, E)]
+            out_shape=[shape(units, heads, UNIT, E)] * 2
+            + [shape(units // 2, heads, UNIT, E)]
             + [shape(rows, width, dtype=BF16)] * 4,
             scratch_shapes=[
                 pltpu.VMEM((3, rows, width), jnp.int32),
@@ -357,7 +357,9 @@
         )(keep, got)
 
     with jax.named_scope("to_owners"):
+        side, g_chip = lax.optimization_barrier((side, g_chip))
         parts = exchange(parts)
+        side_got = lax.ppermute(side, "ctx", swap)
 
     with jax.named_scope("intra"):
         gain_late, parts[0] = lax.optimization_barrier((gain, parts[0]))
@@ -370,6 +372,7 @@
         )(q_spike, k_spike, v_spike, gy, gain_late, g_chip)
 
     with jax.named_scope("to_core"):
+        side_got, g_mine = lax.optimization_barrier((side_got, g_mine))
         pack = pl.pallas_call(
             pack_body,
             out_shape=tiles(4 * heads * near + 1),
@@ -390,8 +393,14 @@
     with jax.named_scope("from_owners"):
         parts = exchange(parts)
 
+    with jax.named_scope("first_states"):
+        first = pl.pallas_call(
+            pack_body, out_shape=tiles(8 * heads + 2), compiler_params=params(2), name="collect_first"
+        )(parts[0], parts[1])
+        first_got = lax.ppermute(first, "ctx", swap)
+
     with jax.named_scope("slopes"):
-        *late, parts[0] = lax.optimization_barrier((q_pre, k_pre, v_pre, parts[0]))
+        *late, first = lax.optimization_barrier((q_pre, k_pre, v_pre, first))
         sq, sk, sv = pl.pallas_call(
             slope_body,
             out_shape=[shape(rows, width)] * 3,
@@ -402,16 +411,17 @@
 
     with jax.named_scope("states"):
         sq, *parts = lax.optimization_barrier((sq, *parts))
-        mine = pl.pallas_call(
+        second = pl.pallas_call(
             collect_body,
-            out_shape=tiles((4 * heads + 1) * near - 2 * heads),
+            out_shape=tiles(6 * heads + 2),
             compiler_params=params(2),
-            name="collect",
-        )(*parts, g_all)
-        theirs = lax.ppermute(mine, "ctx", swap)
+            name="collect_second",
+        )(first, parts[2], parts[3], g_all)
+        second_got = lax.ppermute(second, "ctx", swap)
+        first_got, second_got = lax.optimization_barrier((first_got, second_got))
 
     with jax.named_scope("grad_gain"):
-        g_sum = mine[-1:] + theirs[-1:]
+        g_sum = second[-1:] + second_got[-1:]
         size = lax.axis_size("dp")
         total = g_sum
         for step in range(1, size):
@@ -424,7 +434,7 @@
         whole = pl.BlockSpec(memory_space=pltpu.VMEM)
         grads = pl.pallas_call(
             lambda *refs: finish_body(chips, heads, factor, *refs),
-            in_specs=[whole] * 14,
+            in_specs=[whole] * 17,
             out_specs=[pl.BlockSpec(memory_space=pl.ANY)] * 3,
             out_shape=[shape(1, rows, width, dtype=BF16)] * 3,
             scratch_shapes=[
@@ -434,7 +444,7 @@
             ],
             compiler_params=params(8),
             name="finish",
-        )(mine, theirs, own, got, gain, gy, k_spike, v_spike, dq, dk, dv, sq, sk, sv)
+        )(first, second, first_got, second_got, own, got, side_got, gain, gy, k_spike, v_spike, dq, dk, dv, sq, sk, sv)
     return (*grads, grad_gain)
 
 

time: 57.3 us -> 54.8 us (0.956); the launches traced: 57.2 us -> 54 us
  waiting for transfers between devices: 16.4 us -> 11.2 us
  starting transfers between devices: 22.8 us -> 24.9 us
    ppermute x8, waiting for transfers between devices: 9.71 us -> 5.05 us  [exchange(): lax.ppermute(part, 'ctx', ring(k))]
    ppermute x1 -> x3, starting transfers between devices: 0.09 us -> 2.23 us  [the longest x1 2.05 us: per_device(): side_got = lax.ppermute(side, 'ctx', swap)]
    ppermute x1 -> x3, waiting for transfers between devices: 1.74 us -> 1.41 us  [the longest x1 1.4 us: per_device(): second_got = lax.ppermute(second, 'ctx', swap)]
  transfers between devices with their start and end apart: 14 -> 16, of which waited for: 7 -> 7; matrix products, arithmetic and copies ran while one was open for 0% -> 0% of each run, Pallas kernels for 22% -> 23%
where the time goes in v3:
time: 54.8 us; the launch traced here: 54 us
  starting transfers between devices  24.9 us (45%)
  Pallas kernels  16.5 us (30%)
  waiting for transfers between devices  11.2 us (20%)
  between operations  0.81 us (1%)
  local copies, waits for them, and re-layouts  0.62 us (1%)
    ppermute x8, starting transfers between devices, exchange(): lax.ppermute(part, 'ctx', ring(k))  17.9 us
    pallas_call x1, Pallas kernels, per_device(): pl.pallas_call(lambda *refs: intra_body(heads, factor, *refs), out_shape=...  5.65 us
    ppermute x8, waiting for transfers between devices, exchange(): lax.ppermute(part, 'ctx', ring(k))  5.05 us
    ppermute x3, starting transfers between devices, per_device(): lax.ppermute(g_sum, 'dp', [(i, (i + step) % size) for i in range(size)])  4.45 us
    pallas_call x1, Pallas kernels, per_device(): pl.pallas_call(slope_body, out_shape=[shape(rows, width)] * 3, compiler_p...  3.92 us
    pallas_call x1, Pallas kernels, per_device(): pl.pallas_call(lambda *refs: states_body(chips, heads, factor, *refs), in...  3.79 us
    pallas_call x1, Pallas kernels, per_device(): pl.pallas_call(lambda *refs: finish_body(chips, heads, factor, *refs), in...  2.81 us
    ppermute x1, starting transfers between devices, per_device(): side_got = lax.ppermute(side, 'ctx', swap)  2.05 us
  transfers between devices with their start and end apart: 16, of which 7 were waited for; matrix products, arithmetic and copies ran while one was open for 0% of the time, Pallas kernels for 23%

profile of v3, /device:TPU:16, one launch (start us, length us, event | category | flops | bytes accessed | tf_op | source)
XLA Modules:
  0.0 54.0 jit_solution(8090504989460007762)
XLA Ops:
  0.6 0.0 copy-start
  0.6 3.8 %local_states.1 = (f32[16,7,8,128]{3,2,1,0:T(8,128)S(1)}, f32[16,7,8,128]{3,2,1,0:T(8,128)S(1)}, f32[8,7,8,128]{3,2,1,0:T(8,128)S(1)}, bf16[512,896]{1,0:T(8,128...) custom-call(s32[1,512,896]{2,1,0:T(8,128)} %refs_0_.1, ...), custom_call_target="tpu_custom_call" | custom-call | flops 3000000000 | bytes 6000000 | tf_op jit(solution)/shard_map/local_states/local_states/pallas_call | solution.py:334
  4.4 0.1 collective-permute-start
  4.5 1.8 %collective-permute-done.refs_1_.refs_5_ = f32[16,7,8,128]{3,2,1,0:T(8,128)S(1)} collective-permute-done((f32[16,7,8,128]{3,2,1,0:T(8,128)S(1)}, f32[16,7,8,128]{3,2,1,0:T(8,128)S(1)}, u32[]{:S(2)}, u32[]{:S(2)}) %collective-permute-start) | collective-permute-done | bytes 458784 | tf_op jit(solution)/shard_map/local_states/ppermute | solution.py:349
  6.3 0.1 chip_states.1
  6.4 2.0 %collective-permute-start.1 = (f32[28,8,128]{2,1,0:T(8,128)S(1)}, f32[28,8,128]{2,1,0:T(8,128)S(1)}, u32[]{:S(2)}, u32[]{:S(2)}) collective-permute-start(f32[28,8,128]{2,1,0:T(8,128)S(1)} %get-tuple-element.50), channel_id=1, source_target_pairs={{0,2},{1,15},{2,4},{3,1},{4,6},{5,3},{6,8},{7,5},{8,10},{9,7},{10,... | collective-permute-start | bytes 344072 | tf_op jit(solution)/shard_map/to_owners/ppermute | solution.py:331
  8.4 6.3 %collective-permute-start.4 = (f32[14,8,128]{2,1,0:T(8,128)S(1)}, f32[14,8,128]{2,1,0:T(8,128)S(1)}, u32[]{:S(2)}, u32[]{:S(2)}) collective-permute-start(f32[14,8,128]{2,1,0:T(8,128)S(1)} %get-tuple-element.54), channel_id=1, source_target_pairs={{0,8},{1,9},{2,10},{3,11},{4,12},{5,13},{6,14},{7,15},{8,0},{9,1},... | collective-permute-start | bytes 172040 | tf_op jit(solution)/shard_map/to_owners/ppermute | solution.py:331
  14.7 1.5 %collective-permute-start.2 = (f32[28,8,128]{2,1,0:T(8,128)S(1)}, f32[28,8,128]{2,1,0:T(8,128)S(1)}, u32[]{:S(2)}, u32[]{:S(2)}) collective-permute-start(f32[28,8,128]{2,1,0:T(8,128)S(1)} %get-tuple-element.52), channel_id=1, source_target_pairs={{0,4},{1,13},{2,6},{3,15},{4,8},{5,1},{6,10},{7,3},{8,12},{9,5},{1... | collective-permute-start | bytes 344072 | tf_op jit(solution)/shard_map/to_owners/ppermute | solution.py:331
  16.2 0.1 collective-permute-start.3
  16.3 2.0 %collective-permute-start.5 = (f32[8,7,8,128]{3,2,1,0:T(8,128)S(1)}, f32[8,7,8,128]{3,2,1,0:T(8,128)S(1)}, u32[]{:S(2)}, u32[]{:S(2)}) collective-permute-start(f32[8,7,8,128]{3,2,1,0:T(8,128)S(1)} %get-tuple-element.58), channel_id=1, source_target_pairs={{0,1},{1,0},{2,3},{3,2},{4,5},{5,4},{6,7},{7,6},{8,9},{9,8},{10,11... | collective-permute-start | bytes 688136 | tf_op jit(solution)/shard_map/to_owners/ppermute | solution.py:362
  18.3 0.0 collective-permute-done.1.refs_0_
  18.3 0.0 copy-done
  18.3 0.0 copy-start.3
  18.3 5.7 %intra.1 = (f32[512,896]{1,0:T(8,128)S(1)}, f32[512,896]{1,0:T(8,128)S(1)}, f32[512,896]{1,0:T(8,128)S(1)}, f32[1,8,128]{2,1,0:T(8,128)S(1)}) custom-call(bf16[512,896]{1,0:T(8,128)(2,1)S(1)} %get-tuple-element.59.refs_0_, bf16[512,896]{1,0:T(8,128)(2,1)S(1)} %get-tuple-element.60.refs_1_.refs_9_, bf16[512,896]{1,0:T(8,128)(2,1)S(1)} %get-tuple-element.61.refs_2_.refs_10_, ...), custom_call_target="tpu_custom_call" | custom-call | flops 7000000000 | bytes 14000000 | tf_op jit(solution)/shard_map/intra/intra/pallas_call | solution.py:366
  24.0 0.0 copy-start.1
  24.0 0.0 copy-start.2
  24.0 0.0 collective-permute-done.5.refs_6_
  24.0 0.0 collective-permute-done.4.refs_3_
  24.0 0.0 collective-permute-done.2.refs_1_
  24.0 2.8 %collective-permute-done.3.refs_2_ = f32[28,8,128]{2,1,0:T(8,128)S(1)} collective-permute-done((f32[28,8,128]{2,1,0:T(8,128)S(1)}, f32[28,8,128]{2,1,0:T(8,128)S(1)}, u32[]{:S(2)}, u32[]{:S(2)}) %collective-permute-start.3) | collective-permute-done | bytes 114720 | tf_op jit(solution)/shard_map/to_owners/ppermute | solution.py:331
  26.9 0.3 collective-permute-start.6
  27.1 1.8 %collective-permute-done.6.refs_1_ = f32[113,8,128]{2,1,0:T(8,128)S(1)} collective-permute-done((f32[113,8,128]{2,1,0:T(8,128)S(1)}, f32[113,8,128]{2,1,0:T(8,128)S(1)}, u32[]{:S(2)}, u32[]{:S(2)}) %collective-permute-start.6) | collective-permute-done | bytes 462880 | tf_op jit(solution)/shard_map/to_core/ppermute | solution.py:382
  28.9 0.2 scan.1
  29.1 0.6 %collective-permute-start.7 = (f32[29,8,128]{2,1,0:T(8,128)S(1)}, f32[29,8,128]{2,1,0:T(8,128)S(1)}, u32[]{:S(2)}, u32[]{:S(2)}) collective-permute-start(f32[29,8,128]{2,1,0:T(8,128)S(1)} %get-tuple-element.67), channel_id=1, source_target_pairs={{0,2},{1,15},{2,4},{3,1},{4,6},{5,3},{6,8},{7,5},{8,10},{9,7},{10,... | collective-permute-start | bytes 356360 | tf_op jit(solution)/shard_map/from_owners/ppermute | solution.py:331
  29.7 1.0 %collective-permute-start.8 = (f32[29,8,128]{2,1,0:T(8,128)S(1)}, f32[29,8,128]{2,1,0:T(8,128)S(1)}, u32[]{:S(2)}, u32[]{:S(2)}) collective-permute-start(f32[29,8,128]{2,1,0:T(8,128)S(1)} %get-tuple-element.68), channel_id=1, source_target_pairs={{0,4},{1,13},{2,6},{3,15},{4,8},{5,1},{6,10},{7,3},{8,12},{9,5},{1... | collective-permute-start | bytes 356360 | tf_op jit(solution)/shard_map/from_owners/ppermute | solution.py:331
  30.8 3.2 %collective-permute-start.10 = (f32[15,8,128]{2,1,0:T(8,128)S(1)}, f32[15,8,128]{2,1,0:T(8,128)S(1)}, u32[]{:S(2)}, u32[]{:S(2)}) collective-permute-start(f32[15,8,128]{2,1,0:T(8,128)S(1)} %get-tuple-element.75), channel_id=1, source_target_pairs={{0,8},{1,9},{2,10},{3,11},{4,12},{5,13},{6,14},{7,15},{8,0},{9,1},... | collective-permute-start | bytes 184328 | tf_op jit(solution)/shard_map/from_owners/ppermute | solution.py:331
  34.0 3.2 %collective-permute-start.9 = (f32[29,8,128]{2,1,0:T(8,128)S(1)}, f32[29,8,128]{2,1,0:T(8,128)S(1)}, u32[]{:S(2)}, u32[]{:S(2)}) collective-permute-start(f32[29,8,128]{2,1,0:T(8,128)S(1)} %get-tuple-element.74), channel_id=1, source_target_pairs={{0,6},{1,11},{2,8},{3,13},{4,10},{5,15},{6,12},{7,1},{8,14},{9,3},... | collective-permute-start | bytes 356360 | tf_op jit(solution)/shard_map/from_owners/ppermute | solution.py:331
  37.2 0.0 collective-permute-done.7.refs_0_
  37.2 0.0 collective-permute-done.8.refs_1_
  37.2 0.1 collective-permute-start.11
  37.3 0.0 copy-done.3
  37.3 0.0 copy-done.1
  37.3 0.0 copy-done.2
  37.3 3.9 %slopes.1 = (f32[512,896]{1,0:T(8,128)S(1)}, f32[512,896]{1,0:T(8,128)S(1)}, f32[512,896]{1,0:T(8,128)S(1)}) custom-call(bf16[1,512,896]{2,1,0:T(8,128)(2,1)S(1)} %copy-done.1, bf16[1,512,896]{2,1,0:T(8,128)(2,1)S(1)} %copy-done.2, bf16[1,512,896]{2,1,0:T(8,128)(2,1)S(1)} %copy-done.3), custom_call_target="tpu_custom_call" | custom-call | flops 5000000000 | bytes 10000000 | tf_op jit(solution)/shard_map/slopes/slopes/pallas_call | solution.py:404
  41.3 0.0 collective-permute-done.10.fourth_ref
  41.3 2.2 %collective-permute-done.9.third_ref = f32[29,8,128]{2,1,0:T(8,128)S(1)} collective-permute-done((f32[29,8,128]{2,1,0:T(8,128)S(1)}, f32[29,8,128]{2,1,0:T(8,128)S(1)}, u32[]{:S(2)}, u32[]{:S(2)}) %collective-permute-start.9) | collective-permute-done | bytes 118816 | tf_op jit(solution)/shard_map/from_owners/ppermute | solution.py:331
  43.5 0.1 collective-permute-start.12
  43.6 1.4 %collective-permute-done.12.refs_3_ = f32[44,8,128]{2,1,0:T(8,128)S(1)} collective-permute-done((f32[44,8,128]{2,1,0:T(8,128)S(1)}, f32[44,8,128]{2,1,0:T(8,128)S(1)}, u32[]{:S(2)}, u32[]{:S(2)}) %collective-permute-start.12) | collective-permute-done | bytes 180256 | tf_op jit(solution)/shard_map/states/ppermute | solution.py:420
  45.0 0.0 collective-permute-done.11.refs_2_
  45.0 2.8 %collective-permute-start.15 = (f32[1,8,128]{2,1,0:T(8,128)S(1)}, f32[1,8,128]{2,1,0:T(8,128)S(1)}, u32[]{:S(2)}, u32[]{:S(2)}) collective-permute-start(f32[1,8,128]{2,1,0:T(8,128)S(1)} %slice_add_fusion), channel_id=1, source_target_pairs={{0,192},{64,0},{128,64},{192,128},{1,193},{65,1},{129,65},{193,129... | collective-permute-start | bytes 12296 | tf_op jit(solution)/shard_map/grad_gain/ppermute | solution.py:428
  47.8 0.8 %collective-permute-start.14 = (f32[1,8,128]{2,1,0:T(8,128)S(1)}, f32[1,8,128]{2,1,0:T(8,128)S(1)}, u32[]{:S(2)}, u32[]{:S(2)}) collective-permute-start(f32[1,8,128]{2,1,0:T(8,128)S(1)} %slice_add_fusion), channel_id=1, source_target_pairs={{0,128},{64,192},{128,0},{192,64},{1,129},{65,193},{129,1},{193,65... | collective-permute-start | bytes 12296 | tf_op jit(solution)/shard_map/grad_gain/ppermute | solution.py:428
  48.6 0.9 %collective-permute-start.13 = (f32[1,8,128]{2,1,0:T(8,128)S(1)}, f32[1,8,128]{2,1,0:T(8,128)S(1)}, u32[]{:S(2)}, u32[]{:S(2)}) collective-permute-start(f32[1,8,128]{2,1,0:T(8,128)S(1)} %slice_add_fusion), channel_id=1, source_target_pairs={{0,64},{64,128},{128,192},{192,0},{1,65},{65,129},{129,193},{193,1... | collective-permute-start | bytes 12296 | tf_op jit(solution)/shard_map/grad_gain/ppermute | solution.py:428
  49.5 2.8 %finish.1 = (bf16[1,512,896]{2,1,0:T(8,128)(2,1)}, bf16[1,512,896]{2,1,0:T(8,128)(2,1)}, bf16[1,512,896]{2,1,0:T(8,128)(2,1)}) custom-call(f32[58,8,128]{2,1,0:T(8,128)S(1)} %collect_first.1.first_ref.refs_0_, f32[44,8,128]{2,1,0:T(8,128)S(1)} %collect_second.1.refs_1_, f32[58,8,128]{2,1,0:T(8,128)S(1)} %collective-permute-done.11.refs_2_, ...), custom_call_target="tpu_custom_call" | custom-call | tf_op jit(solution)/shard_map/finish/finish/pallas_call | solution.py:435
  52.3 0.0 collective-permute-done.15
  52.3 0.6 %collective-permute-done.14 = f32[1,8,128]{2,1,0:T(8,128)S(1)} collective-permute-done((f32[1,8,128]{2,1,0:T(8,128)S(1)}, f32[1,8,128]{2,1,0:T(8,128)S(1)}, u32[]{:S(2)}, u32[]{:S(2)}) %collective-permute-start.14) | collective-permute-done | bytes 4128 | tf_op jit(solution)/shard_map/grad_gain/ppermute | solution.py:428
  52.9 0.5 collective-permute-done.13
  53.4 0.6 %slice_bitcast_fusion = f32[896]{0:T(1024)} fusion(f32[1,8,128]{2,1,0:T(8,128)S(1)} %add_add_fusion), kind=kLoop, calls=%fused_computation.1 | loop fusion | bytes 7168 | tf_op jit(solution)/shard_map/grad_gain/reshape;grad_gain/squeeze | solution.py:431
  (5 shorter events, 0.1 us)
Async XLA Ops:
  0.6 17.7 %copy-start = (f32[896]{0:T(1024)S(1)}, f32[896]{0:T(1024)}, u32[]{:S(2)}) copy-start(f32[896]{0:T(1024)} %refs_7_.1) | copy-start | bytes 10756
  4.4 1.9 %collective-permute-start = (f32[16,7,8,128]{3,2,1,0:T(8,128)S(1)}, f32[16,7,8,128]{3,2,1,0:T(8,128)S(1)}, u32[]{:S(2)}, u32[]{:S(2)}) collective-permute-start(f32[16,7,8,128]{3,2,1,0:T(8,128)S(1)} %get-tuple-element.49), channel_id=1, source_target_pairs={{0,1},{1,0},{2,3},{3,2},{4,5},{5,4},{6,7},{7,6},{8,9},{9,8},{10,11... | collective-permute-start | bytes 1376264 | tf_op jit(solution)/shard_map/local_states/ppermute | solution.py:349
  6.4 11.9 %collective-permute-start.1 = (f32[28,8,128]{2,1,0:T(8,128)S(1)}, f32[28,8,128]{2,1,0:T(8,128)S(1)}, u32[]{:S(2)}, u32[]{:S(2)}) collective-permute-start(f32[28,8,128]{2,1,0:T(8,128)S(1)} %get-tuple-element.50), channel_id=1, source_target_pairs={{0,2},{1,15},{2,4},{3,1},{4,6},{5,3},{6,8},{7,5},{8,10},{9,7},{10,... | collective-permute-start | bytes 344072 | tf_op jit(solution)/shard_map/to_owners/ppermute | solution.py:331
  8.4 15.6 %collective-permute-start.4 = (f32[14,8,128]{2,1,0:T(8,128)S(1)}, f32[14,8,128]{2,1,0:T(8,128)S(1)}, u32[]{:S(2)}, u32[]{:S(2)}) collective-permute-start(f32[14,8,128]{2,1,0:T(8,128)S(1)} %get-tuple-element.54), channel_id=1, source_target_pairs={{0,8},{1,9},{2,10},{3,11},{4,12},{5,13},{6,14},{7,15},{8,0},{9,1},... | collective-permute-start | bytes 172040 | tf_op jit(solution)/shard_map/to_owners/ppermute | solution.py:331
  14.7 9.3 %collective-permute-start.2 = (f32[28,8,128]{2,1,0:T(8,128)S(1)}, f32[28,8,128]{2,1,0:T(8,128)S(1)}, u32[]{:S(2)}, u32[]{:S(2)}) collective-permute-start(f32[28,8,128]{2,1,0:T(8,128)S(1)} %get-tuple-element.52), channel_id=1, source_target_pairs={{0,4},{1,13},{2,6},{3,15},{4,8},{5,1},{6,10},{7,3},{8,12},{9,5},{1... | collective-permute-start | bytes 344072 | tf_op jit(solution)/shard_map/to_owners/ppermute | solution.py:331
  16.2 10.7 %collective-permute-start.3 = (f32[28,8,128]{2,1,0:T(8,128)S(1)}, f32[28,8,128]{2,1,0:T(8,128)S(1)}, u32[]{:S(2)}, u32[]{:S(2)}) collective-permute-start(f32[28,8,128]{2,1,0:T(8,128)S(1)} %get-tuple-element.53), channel_id=1, source_target_pairs={{0,6},{1,11},{2,8},{3,13},{4,10},{5,15},{6,12},{7,1},{8,14},{9,3},... | collective-permute-start | bytes 344072 | tf_op jit(solution)/shard_map/to_owners/ppermute | solution.py:331
  16.3 7.7 %collective-permute-start.5 = (f32[8,7,8,128]{3,2,1,0:T(8,128)S(1)}, f32[8,7,8,128]{3,2,1,0:T(8,128)S(1)}, u32[]{:S(2)}, u32[]{:S(2)}) collective-permute-start(f32[8,7,8,128]{3,2,1,0:T(8,128)S(1)} %get-tuple-element.58), channel_id=1, source_target_pairs={{0,1},{1,0},{2,3},{3,2},{4,5},{5,4},{6,7},{7,6},{8,9},{9,8},{10,11... | collective-permute-start | bytes 688136 | tf_op jit(solution)/shard_map/to_owners/ppermute | solution.py:362
  18.3 19.0 %copy-start.3 = (bf16[1,512,896]{2,1,0:T(8,128)(2,1)S(1)}, bf16[1,512,896]{2,1,0:T(8,128)(2,1)}, u32[]{:S(2)}) copy-start(bf16[1,512,896]{2,1,0:T(8,128)(2,1)} %v_ref) | copy-start | bytes 2752516
  24.0 13.4 %copy-start.1 = (bf16[1,512,896]{2,1,0:T(8,128)(2,1)S(1)}, bf16[1,512,896]{2,1,0:T(8,128)(2,1)}, u32[]{:S(2)}) copy-start(bf16[1,512,896]{2,1,0:T(8,128)(2,1)} %q_ref) | copy-start | bytes 2752516
  24.0 13.4 %copy-start.2 = (bf16[1,512,896]{2,1,0:T(8,128)(2,1)S(1)}, bf16[1,512,896]{2,1,0:T(8,128)(2,1)}, u32[]{:S(2)}) copy-start(bf16[1,512,896]{2,1,0:T(8,128)(2,1)} %k_ref) | copy-start | bytes 2752516
  26.9 2.1 %collective-permute-start.6 = (f32[113,8,128]{2,1,0:T(8,128)S(1)}, f32[113,8,128]{2,1,0:T(8,128)S(1)}, u32[]{:S(2)}, u32[]{:S(2)}) collective-permute-start(f32[113,8,128]{2,1,0:T(8,128)S(1)} %pack.1.refs_0_), channel_id=1, source_target_pairs={{0,1},{1,0},{2,3},{3,2},{4,5},{5,4},{6,7},{7,6},{8,9},{9,8},{10,11... | collective-permute-start | bytes 1388552 | tf_op jit(solution)/shard_map/to_core/ppermute | solution.py:382
  29.1 8.0 %collective-permute-start.7 = (f32[29,8,128]{2,1,0:T(8,128)S(1)}, f32[29,8,128]{2,1,0:T(8,128)S(1)}, u32[]{:S(2)}, u32[]{:S(2)}) collective-permute-start(f32[29,8,128]{2,1,0:T(8,128)S(1)} %get-tuple-element.67), channel_id=1, source_target_pairs={{0,2},{1,15},{2,4},{3,1},{4,6},{5,3},{6,8},{7,5},{8,10},{9,7},{10,... | collective-permute-start | bytes 356360 | tf_op jit(solution)/shard_map/from_owners/ppermute | solution.py:331
  29.7 7.5 %collective-permute-start.8 = (f32[29,8,128]{2,1,0:T(8,128)S(1)}, f32[29,8,128]{2,1,0:T(8,128)S(1)}, u32[]{:S(2)}, u32[]{:S(2)}) collective-permute-start(f32[29,8,128]{2,1,0:T(8,128)S(1)} %get-tuple-element.68), channel_id=1, source_target_pairs={{0,4},{1,13},{2,6},{3,15},{4,8},{5,1},{6,10},{7,3},{8,12},{9,5},{1... | collective-permute-start | bytes 356360 | tf_op jit(solution)/shard_map/from_owners/ppermute | solution.py:331
  30.8 10.5 %collective-permute-start.10 = (f32[15,8,128]{2,1,0:T(8,128)S(1)}, f32[15,8,128]{2,1,0:T(8,128)S(1)}, u32[]{:S(2)}, u32[]{:S(2)}) collective-permute-start(f32[15,8,128]{2,1,0:T(8,128)S(1)} %get-tuple-element.75), channel_id=1, source_target_pairs={{0,8},{1,9},{2,10},{3,11},{4,12},{5,13},{6,14},{7,15},{8,0},{9,1},... | collective-permute-start | bytes 184328 | tf_op jit(solution)/shard_map/from_owners/ppermute | solution.py:331
  34.0 9.5 %collective-permute-start.9 = (f32[29,8,128]{2,1,0:T(8,128)S(1)}, f32[29,8,128]{2,1,0:T(8,128)S(1)}, u32[]{:S(2)}, u32[]{:S(2)}) collective-permute-start(f32[29,8,128]{2,1,0:T(8,128)S(1)} %get-tuple-element.74), channel_id=1, source_target_pairs={{0,6},{1,11},{2,8},{3,13},{4,10},{5,15},{6,12},{7,1},{8,14},{9,3},... | collective-permute-start | bytes 356360 | tf_op jit(solution)/shard_map/from_owners/ppermute | solution.py:331
  37.2 7.8 %collective-permute-start.11 = (f32[58,8,128]{2,1,0:T(8,128)S(1)}, f32[58,8,128]{2,1,0:T(8,128)S(1)}, u32[]{:S(2)}, u32[]{:S(2)}) collective-permute-start(f32[58,8,128]{2,1,0:T(8,128)S(1)} %collect_first.1.first_ref.refs_0_), channel_id=1, source_target_pairs={{0,1},{1,0},{2,3},{3,2},{4,5},{5,4},{6,7},{7,6},{8,9},{9,8},{10,11... | collective-permute-start | bytes 712712 | tf_op jit(solution)/shard_map/first_states/ppermute | solution.py:400
  43.5 1.5 %collective-permute-start.12 = (f32[44,8,128]{2,1,0:T(8,128)S(1)}, f32[44,8,128]{2,1,0:T(8,128)S(1)}, u32[]{:S(2)}, u32[]{:S(2)}) collective-permute-start(f32[44,8,128]{2,1,0:T(8,128)S(1)} %collect_second.1.refs_1_), channel_id=1, source_target_pairs={{0,1},{1,0},{2,3},{3,2},{4,5},{5,4},{6,7},{7,6},{8,9},{9,8},{10,11... | collective-permute-start | bytes 540680 | tf_op jit(solution)/shard_map/states/ppermute | solution.py:420
  45.0 7.3 %collective-permute-start.15 = (f32[1,8,128]{2,1,0:T(8,128)S(1)}, f32[1,8,128]{2,1,0:T(8,128)S(1)}, u32[]{:S(2)}, u32[]{:S(2)}) collective-permute-start(f32[1,8,128]{2,1,0:T(8,128)S(1)} %slice_add_fusion), channel_id=1, source_target_pairs={{0,192},{64,0},{128,64},{192,128},{1,193},{65,1},{129,65},{193,129... | collective-permute-start | bytes 12296 | tf_op jit(solution)/shard_map/grad_gain/ppermute | solution.py:428
  47.8 5.1 %collective-permute-start.14 = (f32[1,8,128]{2,1,0:T(8,128)S(1)}, f32[1,8,128]{2,1,0:T(8,128)S(1)}, u32[]{:S(2)}, u32[]{:S(2)}) collective-permute-start(f32[1,8,128]{2,1,0:T(8,128)S(1)} %slice_add_fusion), channel_id=1, source_target_pairs={{0,128},{64,192},{128,0},{192,64},{1,129},{65,193},{129,1},{193,65... | collective-permute-start | bytes 12296 | tf_op jit(solution)/shard_map/grad_gain/ppermute | solution.py:428
  48.6 4.8 %collective-permute-start.13 = (f32[1,8,128]{2,1,0:T(8,128)S(1)}, f32[1,8,128]{2,1,0:T(8,128)S(1)}, u32[]{:S(2)}, u32[]{:S(2)}) collective-permute-start(f32[1,8,128]{2,1,0:T(8,128)S(1)} %slice_add_fusion), channel_id=1, source_target_pairs={{0,64},{64,128},{128,192},{192,0},{1,65},{65,129},{129,193},{193,1... | collective-permute-start | bytes 12296 | tf_op jit(solution)/shard_map/grad_gain/ppermute | solution.py:428

commit v4 on v3

--- a/solution.py
+++ b/solution.py
@@ -112,16 +112,16 @@
     g_ref[0, 0:heads] = jnp.sum(cross, axis=1)
 
 
-def scan_body(chips, heads, x_ref, y_ref, o1_ref, o2_ref, o3_ref, o4_ref, own_ref, g_ref, have, give):
+def scan_body(chips, heads, x1_ref, x2_ref, y1_ref, y2_ref, o1_ref, o2_ref, o3_ref, o4_ref, own_ref, g_ref, have, give):
     chip, core, way = place()
     wide, near = 4 * heads, chips // 2
-    for ref, go, lane in ((x_ref, way, core), (y_ref, -way, 1 - core)):
-        for k in range(1, near):
+    both = ((x1_ref, x2_ref, way, core), (y1_ref, y2_ref, -way, 1 - core))
+    for one_ref, two_ref, go, lane in both:
+        for k, ref, base in ((1, one_ref, 0), (2, one_ref, wide), (3, two_ref, 0)):
             at = around(chip, -go * k, chips)
-            have[at] = ref[wide * (k - 1) : wide * k].reshape(2, 2 * heads, UNIT, E)
-        base = wide * (near - 1)
-        have[around(chip, near, chips), lane] = ref[base : base + 2 * heads]
-        have[chip, lane] = ref[base + 2 * heads : base + 4 * heads]
+            have[at] = ref[base : base + wide].reshape(2, 2 * heads, UNIT, E)
+        have[chip, lane] = one_ref[2 * wide :]
+        have[around(chip, near, chips), lane] = two_ref[wide : wide + 2 * heads]
     zero = jnp.zeros((2, heads, UNIT, E), F32)
     before, after, cross = zero, zero, zero
     for i in range(chips):
@@ -131,8 +131,8 @@
     for i in reversed(range(chips)):
         give[i, :, heads : 2 * heads] = after
         after = after + have[i, :, heads : 2 * heads]
-    last = wide * near
-    g_ref[...] = x_ref[last : last + 1] + y_ref[last : last + 1]
+    last = wide + 2 * heads
+    g_ref[...] = x2_ref[last:] + y2_ref[last:]
     g_ref[0, 0:heads] = g_ref[0, 0:heads] + jnp.sum(cross[0] + cross[1], axis=1)
     for k, ref in ((1, o1_ref), (2, o2_ref), (3, o3_ref)):
         ref[0:wide] = give[around(chip, way * k, chips)].reshape(wide, UNIT, E)
@@ -357,9 +357,7 @@
         )(keep, got)
 
     with jax.named_scope("to_owners"):
-        side, g_chip = lax.optimization_barrier((side, g_chip))
         parts = exchange(parts)
-        side_got = lax.ppermute(side, "ctx", swap)
 
     with jax.named_scope("intra"):
         gain_late, parts[0] = lax.optimization_barrier((gain, parts[0]))
@@ -372,14 +370,14 @@
         )(q_spike, k_spike, v_spike, gy, gain_late, g_chip)
 
     with jax.named_scope("to_core"):
-        side_got, g_mine = lax.optimization_barrier((side_got, g_mine))
-        pack = pl.pallas_call(
-            pack_body,
-            out_shape=tiles(4 * heads * near + 1),
-            compiler_params=params(2),
-            name="pack",
-        )(*parts, own, g_mine)
-        pack_got = lax.ppermute(pack, "ctx", swap)
+        first = pl.pallas_call(
+            pack_body, out_shape=tiles(10 * heads), compiler_params=params(2), name="pack_first"
+        )(parts[0], parts[1], own)
+        first_got = lax.ppermute(first, "ctx", swap)
+        second = pl.pallas_call(
+            pack_body, out_shape=tiles(6 * heads + 1), compiler_params=params(2), name="pack_second"
+        )(parts[2], parts[3], g_mine)
+        second_got = lax.ppermute(second, "ctx", swap)
 
     with jax.named_scope("scan"):
         *parts, own, g_all = pl.pallas_call(
@@ -388,10 +386,14 @@
             scratch_shapes=[pltpu.VMEM((chips, 2, 2 * heads, UNIT, E), F32)] * 2,
             compiler_params=params(4),
             name="scan",
-        )(pack, pack_got)
+        )(first, second, first_got, second_got)
 
     with jax.named_scope("from_owners"):
         parts = exchange(parts)
+
+    with jax.named_scope("side_states"):
+        side, g_all = lax.optimization_barrier((side, g_all))
+        side_got = lax.ppermute(side, "ctx", swap)
 
     with jax.named_scope("first_states"):
         first = pl.pallas_call(
@@ -410,7 +412,7 @@
         )(*late)
 
     with jax.named_scope("states"):
-        sq, *parts = lax.optimization_barrier((sq, *parts))
+        sq, side_got, *parts = lax.optimization_barrier((sq, side_got, *parts))
         second = pl.pallas_call(
             collect_body,
             out_shape=tiles(6 * heads + 2),

time: 54.8 us -> 56.8 us (1.036); the launches traced: 54 us -> 56.7 us
  waiting for transfers between devices: 11.2 us -> 14.6 us
  starting transfers between devices: 24.9 us -> 24.1 us
    ppermute x8, waiting for transfers between devices: 5.05 us -> 8.83 us  [exchange(): lax.ppermute(part, 'ctx', ring(k))]
    ppermute x1 -> x0, waiting for transfers between devices: 1.81 us -> none  [per_device(): pack_got = lax.ppermute(pack, 'ctx', swap)]
    ppermute x1 -> x2, waiting for transfers between devices: 1.4 us -> 2.79 us  [per_device(): second_got = lax.ppermute(second, 'ctx', swap)]
    ppermute x1, starting transfers between devices: 2.05 us -> 1.2 us  [per_device(): side_got = lax.ppermute(side, 'ctx', swap)]
  transfers between devices with their start and end apart: 16 -> 17, of which waited for: 7 -> 9; matrix products, arithmetic and copies ran while one was open for 0% -> 0% of each run, Pallas kernels for 23% -> 22%
where the time goes in v4:
time: 56.8 us; the launch traced here: 56.7 us
  starting transfers between devices  24.1 us (42%)
  Pallas kernels  16.5 us (29%)
  waiting for transfers between devices  14.6 us (26%)
  between operations  0.83 us (1%)
  local copies, waits for them, and re-layouts  0.62 us (1%)
    ppermute x8, starting transfers between devices, exchange(): lax.ppermute(part, 'ctx', ring(k))  17.7 us
    ppermute x8, waiting for transfers between devices, exchange(): lax.ppermute(part, 'ctx', ring(k))  8.83 us
    pallas_call x1, Pallas kernels, per_device(): pl.pallas_call(lambda *refs: intra_body(heads, factor, *refs), out_shape=...  5.65 us
    ppermute x3, starting transfers between devices, per_device(): lax.ppermute(g_sum, 'dp', [(i, (i + step) % size) for i in range(size)])  4.58 us
    pallas_call x1, Pallas kernels, per_device(): pl.pallas_call(slope_body, out_shape=[shape(rows, width)] * 3, compiler_p...  3.92 us
    pallas_call x1, Pallas kernels, per_device(): pl.pallas_call(lambda *refs: states_body(chips, heads, factor, *refs), in...  3.79 us
    pallas_call x1, Pallas kernels, per_device(): pl.pallas_call(lambda *refs: finish_body(chips, heads, factor, *refs), in...  2.81 us
    ppermute x2, waiting for transfers between devices, per_device(): second_got = lax.ppermute(second, 'ctx', swap)  2.79 us
  transfers between devices with their start and end apart: 17, of which 9 were waited for; matrix products, arithmetic and copies ran while one was open for 0% of the time, Pallas kernels for 22%

profile of v4, /device:TPU:16, one launch (start us, length us, event | category | flops | bytes accessed | tf_op | source)
XLA Modules:
  0.0 56.7 jit_solution(12404046568627067230)
XLA Ops:
  0.6 0.0 copy-start
  0.6 3.8 %local_states.1 = (f32[16,7,8,128]{3,2,1,0:T(8,128)S(1)}, f32[16,7,8,128]{3,2,1,0:T(8,128)S(1)}, f32[8,7,8,128]{3,2,1,0:T(8,128)S(1)}, bf16[512,896]{1,0:T(8,128...) custom-call(s32[1,512,896]{2,1,0:T(8,128)} %refs_0_.1, ...), custom_call_target="tpu_custom_call" | custom-call | flops 3000000000 | bytes 6000000 | tf_op jit(solution)/shard_map/local_states/local_states/pallas_call | solution.py:334
  4.4 0.1 collective-permute-start
  4.5 1.8 %collective-permute-done.refs_1_.refs_5_ = f32[16,7,8,128]{3,2,1,0:T(8,128)S(1)} collective-permute-done((f32[16,7,8,128]{3,2,1,0:T(8,128)S(1)}, f32[16,7,8,128]{3,2,1,0:T(8,128)S(1)}, u32[]{:S(2)}, u32[]{:S(2)}) %collective-permute-start) | collective-permute-done | bytes 458784 | tf_op jit(solution)/shard_map/local_states/ppermute | solution.py:349
  6.3 0.1 chip_states.1
  6.4 2.0 %collective-permute-start.1 = (f32[28,8,128]{2,1,0:T(8,128)S(1)}, f32[28,8,128]{2,1,0:T(8,128)S(1)}, u32[]{:S(2)}, u32[]{:S(2)}) collective-permute-start(f32[28,8,128]{2,1,0:T(8,128)S(1)} %get-tuple-element.49), channel_id=1, source_target_pairs={{0,2},{1,15},{2,4},{3,1},{4,6},{5,3},{6,8},{7,5},{8,10},{9,7},{10,... | collective-permute-start | bytes 344072 | tf_op jit(solution)/shard_map/to_owners/ppermute | solution.py:331
  8.4 3.3 %collective-permute-start.2 = (f32[28,8,128]{2,1,0:T(8,128)S(1)}, f32[28,8,128]{2,1,0:T(8,128)S(1)}, u32[]{:S(2)}, u32[]{:S(2)}) collective-permute-start(f32[28,8,128]{2,1,0:T(8,128)S(1)} %get-tuple-element.51), channel_id=1, source_target_pairs={{0,4},{1,13},{2,6},{3,15},{4,8},{5,1},{6,10},{7,3},{8,12},{9,5},{1... | collective-permute-start | bytes 344072 | tf_op jit(solution)/shard_map/to_owners/ppermute | solution.py:331
  11.7 4.5 %collective-permute-start.4 = (f32[14,8,128]{2,1,0:T(8,128)S(1)}, f32[14,8,128]{2,1,0:T(8,128)S(1)}, u32[]{:S(2)}, u32[]{:S(2)}) collective-permute-start(f32[14,8,128]{2,1,0:T(8,128)S(1)} %get-tuple-element.54), channel_id=1, source_target_pairs={{0,8},{1,9},{2,10},{3,11},{4,12},{5,13},{6,14},{7,15},{8,0},{9,1},... | collective-permute-start | bytes 172040 | tf_op jit(solution)/shard_map/to_owners/ppermute | solution.py:331
  16.2 0.1 collective-permute-start.3
  16.3 0.0 collective-permute-done.1.refs_0_
  16.3 2.3 %collective-permute-done.2.refs_1_ = f32[28,8,128]{2,1,0:T(8,128)S(1)} collective-permute-done((f32[28,8,128]{2,1,0:T(8,128)S(1)}, f32[28,8,128]{2,1,0:T(8,128)S(1)}, u32[]{:S(2)}, u32[]{:S(2)}) %collective-permute-start.2) | collective-permute-done | bytes 114720 | tf_op jit(solution)/shard_map/to_owners/ppermute | solution.py:331
  18.6 0.1 collective-permute-start.5
  18.7 0.0 copy-done
  18.7 0.0 copy-start.1
  18.7 0.0 copy-start.2
  18.8 0.0 copy-start.3
  18.8 5.7 %intra.1 = (f32[512,896]{1,0:T(8,128)S(1)}, f32[512,896]{1,0:T(8,128)S(1)}, f32[512,896]{1,0:T(8,128)S(1)}, f32[1,8,128]{2,1,0:T(8,128)S(1)}) custom-call(bf16[512,896]{1,0:T(8,128)(2,1)S(1)} %get-tuple-element.55.refs_0_, bf16[512,896]{1,0:T(8,128)(2,1)S(1)} %get-tuple-element.56.refs_1_.refs_9_, bf16[512,896]{1,0:T(8,128)(2,1)S(1)} %get-tuple-element.57.refs_2_.refs_10_, ...), custom_call_target="tpu_custom_call" | custom-call | flops 7000000000 | bytes 14000000 | tf_op jit(solution)/shard_map/intra/intra/pallas_call | solution.py:364
  24.4 0.0 collective-permute-done.4.refs_1_
  24.4 2.0 %collective-permute-done.3.refs_0_ = f32[28,8,128]{2,1,0:T(8,128)S(1)} collective-permute-done((f32[28,8,128]{2,1,0:T(8,128)S(1)}, f32[28,8,128]{2,1,0:T(8,128)S(1)}, u32[]{:S(2)}, u32[]{:S(2)}) %collective-permute-start.3) | collective-permute-done | bytes 114720 | tf_op jit(solution)/shard_map/to_owners/ppermute | solution.py:331
  26.4 0.3 collective-permute-start.6
  26.7 1.4 %collective-permute-done.6.refs_3_ = f32[43,8,128]{2,1,0:T(8,128)S(1)} collective-permute-done((f32[43,8,128]{2,1,0:T(8,128)S(1)}, f32[43,8,128]{2,1,0:T(8,128)S(1)}, u32[]{:S(2)}, u32[]{:S(2)}) %collective-permute-start.6) | collective-permute-done | bytes 176160 | tf_op jit(solution)/shard_map/to_core/ppermute | solution.py:380
  28.1 0.0 collective-permute-done.5.refs_2_
  28.1 0.2 scan.1
  28.3 0.3 collective-permute-start.7
  28.6 1.2 %collective-permute-start.8 = (f32[29,8,128]{2,1,0:T(8,128)S(1)}, f32[29,8,128]{2,1,0:T(8,128)S(1)}, u32[]{:S(2)}, u32[]{:S(2)}) collective-permute-start(f32[29,8,128]{2,1,0:T(8,128)S(1)} %get-tuple-element.63), channel_id=1, source_target_pairs={{0,4},{1,13},{2,6},{3,15},{4,8},{5,1},{6,10},{7,3},{8,12},{9,5},{1... | collective-permute-start | bytes 356360 | tf_op jit(solution)/shard_map/from_owners/ppermute | solution.py:331
  29.7 5.5 %collective-permute-start.11 = (f32[15,8,128]{2,1,0:T(8,128)S(1)}, f32[15,8,128]{2,1,0:T(8,128)S(1)}, u32[]{:S(2)}, u32[]{:S(2)}) collective-permute-start(f32[15,8,128]{2,1,0:T(8,128)S(1)} %get-tuple-element.73), channel_id=1, source_target_pairs={{0,8},{1,9},{2,10},{3,11},{4,12},{5,13},{6,14},{7,15},{8,0},{9,1},... | collective-permute-start | bytes 184328 | tf_op jit(solution)/shard_map/from_owners/ppermute | solution.py:331
  35.3 0.9 %collective-permute-start.10 = (f32[29,8,128]{2,1,0:T(8,128)S(1)}, f32[29,8,128]{2,1,0:T(8,128)S(1)}, u32[]{:S(2)}, u32[]{:S(2)}) collective-permute-start(f32[29,8,128]{2,1,0:T(8,128)S(1)} %get-tuple-element.72), channel_id=1, source_target_pairs={{0,6},{1,11},{2,8},{3,13},{4,10},{5,15},{6,12},{7,1},{8,14},{9,3},... | collective-permute-start | bytes 356360 | tf_op jit(solution)/shard_map/from_owners/ppermute | solution.py:331
  36.1 1.2 %collective-permute-start.9 = (f32[8,7,8,128]{3,2,1,0:T(8,128)S(1)}, f32[8,7,8,128]{3,2,1,0:T(8,128)S(1)}, u32[]{:S(2)}, u32[]{:S(2)}) collective-permute-start(f32[8,7,8,128]{3,2,1,0:T(8,128)S(1)} %get-tuple-element.71), channel_id=1, source_target_pairs={{0,1},{1,0},{2,3},{3,2},{4,5},{5,4},{6,7},{7,6},{8,9},{9,8},{10,11... | collective-permute-start | bytes 688136 | tf_op jit(solution)/shard_map/side_states/ppermute | solution.py:396
  37.3 0.0 collective-permute-done.7.refs_0_
  37.4 0.4 collective-permute-done.8.refs_1_
  37.8 0.1 collective-permute-start.12
  37.9 0.0 copy-done.1
  37.9 0.0 copy-done.2
  37.9 0.0 copy-done.3
  37.9 3.9 %slopes.1 = (f32[512,896]{1,0:T(8,128)S(1)}, f32[512,896]{1,0:T(8,128)S(1)}, f32[512,896]{1,0:T(8,128)S(1)}) custom-call(bf16[1,512,896]{2,1,0:T(8,128)(2,1)S(1)} %copy-done.1, bf16[1,512,896]{2,1,0:T(8,128)(2,1)S(1)} %copy-done.2, bf16[1,512,896]{2,1,0:T(8,128)(2,1)S(1)} %copy-done.3), custom_call_target="tpu_custom_call" | custom-call | flops 5000000000 | bytes 10000000 | tf_op jit(solution)/shard_map/slopes/slopes/pallas_call | solution.py:406
  41.9 0.0 collective-permute-done.11.fourth_ref
  41.9 4.1 %collective-permute-done.10.third_ref = f32[29,8,128]{2,1,0:T(8,128)S(1)} collective-permute-done((f32[29,8,128]{2,1,0:T(8,128)S(1)}, f32[29,8,128]{2,1,0:T(8,128)S(1)}, u32[]{:S(2)}, u32[]{:S(2)}) %collective-permute-start.10) | collective-permute-done | bytes 118816 | tf_op jit(solution)/shard_map/from_owners/ppermute | solution.py:331
  46.0 0.0 collective-permute-done.9.refs_6_
  46.0 0.1 collective-permute-start.13
  46.1 0.0 collective-permute-done.12.refs_2_
  46.1 1.4 %collective-permute-done.13.refs_3_ = f32[44,8,128]{2,1,0:T(8,128)S(1)} collective-permute-done((f32[44,8,128]{2,1,0:T(8,128)S(1)}, f32[44,8,128]{2,1,0:T(8,128)S(1)}, u32[]{:S(2)}, u32[]{:S(2)}) %collective-permute-start.13) | collective-permute-done | bytes 180256 | tf_op jit(solution)/shard_map/states/ppermute | solution.py:422
  47.5 2.8 %collective-permute-start.16 = (f32[1,8,128]{2,1,0:T(8,128)S(1)}, f32[1,8,128]{2,1,0:T(8,128)S(1)}, u32[]{:S(2)}, u32[]{:S(2)}) collective-permute-start(f32[1,8,128]{2,1,0:T(8,128)S(1)} %slice_add_fusion), channel_id=1, source_target_pairs={{0,192},{64,0},{128,64},{192,128},{1,193},{65,1},{129,65},{193,129... | collective-permute-start | bytes 12296 | tf_op jit(solution)/shard_map/grad_gain/ppermute | solution.py:430
  50.3 1.0 %collective-permute-start.15 = (f32[1,8,128]{2,1,0:T(8,128)S(1)}, f32[1,8,128]{2,1,0:T(8,128)S(1)}, u32[]{:S(2)}, u32[]{:S(2)}) collective-permute-start(f32[1,8,128]{2,1,0:T(8,128)S(1)} %slice_add_fusion), channel_id=1, source_target_pairs={{0,128},{64,192},{128,0},{192,64},{1,129},{65,193},{129,1},{193,65... | collective-permute-start | bytes 12296 | tf_op jit(solution)/shard_map/grad_gain/ppermute | solution.py:430
  51.3 0.8 %collective-permute-start.14 = (f32[1,8,128]{2,1,0:T(8,128)S(1)}, f32[1,8,128]{2,1,0:T(8,128)S(1)}, u32[]{:S(2)}, u32[]{:S(2)}) collective-permute-start(f32[1,8,128]{2,1,0:T(8,128)S(1)} %slice_add_fusion), channel_id=1, source_target_pairs={{0,64},{64,128},{128,192},{192,0},{1,65},{65,129},{129,193},{193,1... | collective-permute-start | bytes 12296 | tf_op jit(solution)/shard_map/grad_gain/ppermute | solution.py:430
  52.1 2.8 %finish.1 = (bf16[1,512,896]{2,1,0:T(8,128)(2,1)}, bf16[1,512,896]{2,1,0:T(8,128)(2,1)}, bf16[1,512,896]{2,1,0:T(8,128)(2,1)}) custom-call(f32[58,8,128]{2,1,0:T(8,128)S(1)} %collect_first.1.first_ref.refs_0_, f32[44,8,128]{2,1,0:T(8,128)S(1)} %collect_second.1.refs_1_, f32[58,8,128]{2,1,0:T(8,128)S(1)} %collective-permute-done.12.refs_2_, ...), custom_call_target="tpu_custom_call" | custom-call | tf_op jit(solution)/shard_map/finish/finish/pallas_call | solution.py:437
  54.9 0.0 collective-permute-done.16
  54.9 0.5 collective-permute-done.15
  55.4 0.7 %collective-permute-done.14 = f32[1,8,128]{2,1,0:T(8,128)S(1)} collective-permute-done((f32[1,8,128]{2,1,0:T(8,128)S(1)}, f32[1,8,128]{2,1,0:T(8,128)S(1)}, u32[]{:S(2)}, u32[]{:S(2)}) %collective-permute-start.14) | collective-permute-done | bytes 4128 | tf_op jit(solution)/shard_map/grad_gain/ppermute | solution.py:430
  56.1 0.6 %slice_bitcast_fusion = f32[896]{0:T(1024)} fusion(f32[1,8,128]{2,1,0:T(8,128)S(1)} %add_add_fusion), kind=kLoop, calls=%fused_computation.1 | loop fusion | bytes 7168 | tf_op jit(solution)/shard_map/grad_gain/reshape;grad_gain/squeeze | solution.py:433
  (6 shorter events, 0.1 us)
Async XLA Ops:
  0.6 18.1 %copy-start = (f32[896]{0:T(1024)S(1)}, f32[896]{0:T(1024)}, u32[]{:S(2)}) copy-start(f32[896]{0:T(1024)} %refs_7_.1) | copy-start | bytes 10756
  4.4 1.9 %collective-permute-start = (f32[16,7,8,128]{3,2,1,0:T(8,128)S(1)}, f32[16,7,8,128]{3,2,1,0:T(8,128)S(1)}, u32[]{:S(2)}, u32[]{:S(2)}) collective-permute-start(f32[16,7,8,128]{3,2,1,0:T(8,128)S(1)} %get-tuple-element.48), channel_id=1, source_target_pairs={{0,1},{1,0},{2,3},{3,2},{4,5},{5,4},{6,7},{7,6},{8,9},{9,8},{10,11... | collective-permute-start | bytes 1376264 | tf_op jit(solution)/shard_map/local_states/ppermute | solution.py:349
  6.4 9.8 %collective-permute-start.1 = (f32[28,8,128]{2,1,0:T(8,128)S(1)}, f32[28,8,128]{2,1,0:T(8,128)S(1)}, u32[]{:S(2)}, u32[]{:S(2)}) collective-permute-start(f32[28,8,128]{2,1,0:T(8,128)S(1)} %get-tuple-element.49), channel_id=1, source_target_pairs={{0,2},{1,15},{2,4},{3,1},{4,6},{5,3},{6,8},{7,5},{8,10},{9,7},{10,... | collective-permute-start | bytes 344072 | tf_op jit(solution)/shard_map/to_owners/ppermute | solution.py:331
  8.4 10.2 %collective-permute-start.2 = (f32[28,8,128]{2,1,0:T(8,128)S(1)}, f32[28,8,128]{2,1,0:T(8,128)S(1)}, u32[]{:S(2)}, u32[]{:S(2)}) collective-permute-start(f32[28,8,128]{2,1,0:T(8,128)S(1)} %get-tuple-element.51), channel_id=1, source_target_pairs={{0,4},{1,13},{2,6},{3,15},{4,8},{5,1},{6,10},{7,3},{8,12},{9,5},{1... | collective-permute-start | bytes 344072 | tf_op jit(solution)/shard_map/to_owners/ppermute | solution.py:331
  11.7 12.7 %collective-permute-start.4 = (f32[14,8,128]{2,1,0:T(8,128)S(1)}, f32[14,8,128]{2,1,0:T(8,128)S(1)}, u32[]{:S(2)}, u32[]{:S(2)}) collective-permute-start(f32[14,8,128]{2,1,0:T(8,128)S(1)} %get-tuple-element.54), channel_id=1, source_target_pairs={{0,8},{1,9},{2,10},{3,11},{4,12},{5,13},{6,14},{7,15},{8,0},{9,1},... | collective-permute-start | bytes 172040 | tf_op jit(solution)/shard_map/to_owners/ppermute | solution.py:331
  16.2 10.2 %collective-permute-start.3 = (f32[28,8,128]{2,1,0:T(8,128)S(1)}, f32[28,8,128]{2,1,0:T(8,128)S(1)}, u32[]{:S(2)}, u32[]{:S(2)}) collective-permute-start(f32[28,8,128]{2,1,0:T(8,128)S(1)} %get-tuple-element.53), channel_id=1, source_target_pairs={{0,6},{1,11},{2,8},{3,13},{4,10},{5,15},{6,12},{7,1},{8,14},{9,3},... | collective-permute-start | bytes 344072 | tf_op jit(solution)/shard_map/to_owners/ppermute | solution.py:331
  18.6 9.5 %collective-permute-start.5 = (f32[70,8,128]{2,1,0:T(8,128)S(1)}, f32[70,8,128]{2,1,0:T(8,128)S(1)}, u32[]{:S(2)}, u32[]{:S(2)}) collective-permute-start(f32[70,8,128]{2,1,0:T(8,128)S(1)} %pack_first.1.refs_0_), channel_id=1, source_target_pairs={{0,1},{1,0},{2,3},{3,2},{4,5},{5,4},{6,7},{7,6},{8,9},{9,8},{10,11... | collective-permute-start | bytes 860168 | tf_op jit(solution)/shard_map/to_core/ppermute | solution.py:376
  18.7 19.2 %copy-start.1 = (bf16[1,512,896]{2,1,0:T(8,128)(2,1)S(1)}, bf16[1,512,896]{2,1,0:T(8,128)(2,1)}, u32[]{:S(2)}) copy-start(bf16[1,512,896]{2,1,0:T(8,128)(2,1)} %q_ref) | copy-start | bytes 2752516
  18.7 19.2 %copy-start.2 = (bf16[1,512,896]{2,1,0:T(8,128)(2,1)S(1)}, bf16[1,512,896]{2,1,0:T(8,128)(2,1)}, u32[]{:S(2)}) copy-start(bf16[1,512,896]{2,1,0:T(8,128)(2,1)} %k_ref) | copy-start | bytes 2752516
  18.8 19.2 %copy-start.3 = (bf16[1,512,896]{2,1,0:T(8,128)(2,1)S(1)}, bf16[1,512,896]{2,1,0:T(8,128)(2,1)}, u32[]{:S(2)}) copy-start(bf16[1,512,896]{2,1,0:T(8,128)(2,1)} %v_ref) | copy-start | bytes 2752516
  26.4 1.7 %collective-permute-start.6 = (f32[43,8,128]{2,1,0:T(8,128)S(1)}, f32[43,8,128]{2,1,0:T(8,128)S(1)}, u32[]{:S(2)}, u32[]{:S(2)}) collective-permute-start(f32[43,8,128]{2,1,0:T(8,128)S(1)} %pack_second.1.refs_1_), channel_id=1, source_target_pairs={{0,1},{1,0},{2,3},{3,2},{4,5},{5,4},{6,7},{7,6},{8,9},{9,8},{10,11... | collective-permute-start | bytes 528392 | tf_op jit(solution)/shard_map/to_core/ppermute | solution.py:380
  28.3 9.1 %collective-permute-start.7 = (f32[29,8,128]{2,1,0:T(8,128)S(1)}, f32[29,8,128]{2,1,0:T(8,128)S(1)}, u32[]{:S(2)}, u32[]{:S(2)}) collective-permute-start(f32[29,8,128]{2,1,0:T(8,128)S(1)} %get-tuple-element.62), channel_id=1, source_target_pairs={{0,2},{1,15},{2,4},{3,1},{4,6},{5,3},{6,8},{7,5},{8,10},{9,7},{10,... | collective-permute-start | bytes 356360 | tf_op jit(solution)/shard_map/from_owners/ppermute | solution.py:331
  28.6 9.2 %collective-permute-start.8 = (f32[29,8,128]{2,1,0:T(8,128)S(1)}, f32[29,8,128]{2,1,0:T(8,128)S(1)}, u32[]{:S(2)}, u32[]{:S(2)}) collective-permute-start(f32[29,8,128]{2,1,0:T(8,128)S(1)} %get-tuple-element.63), channel_id=1, source_target_pairs={{0,4},{1,13},{2,6},{3,15},{4,8},{5,1},{6,10},{7,3},{8,12},{9,5},{1... | collective-permute-start | bytes 356360 | tf_op jit(solution)/shard_map/from_owners/ppermute | solution.py:331
  29.7 12.1 %collective-permute-start.11 = (f32[15,8,128]{2,1,0:T(8,128)S(1)}, f32[15,8,128]{2,1,0:T(8,128)S(1)}, u32[]{:S(2)}, u32[]{:S(2)}) collective-permute-start(f32[15,8,128]{2,1,0:T(8,128)S(1)} %get-tuple-element.73), channel_id=1, source_target_pairs={{0,8},{1,9},{2,10},{3,11},{4,12},{5,13},{6,14},{7,15},{8,0},{9,1},... | collective-permute-start | bytes 184328 | tf_op jit(solution)/shard_map/from_owners/ppermute | solution.py:331
  35.3 10.7 %collective-permute-start.10 = (f32[29,8,128]{2,1,0:T(8,128)S(1)}, f32[29,8,128]{2,1,0:T(8,128)S(1)}, u32[]{:S(2)}, u32[]{:S(2)}) collective-permute-start(f32[29,8,128]{2,1,0:T(8,128)S(1)} %get-tuple-element.72), channel_id=1, source_target_pairs={{0,6},{1,11},{2,8},{3,13},{4,10},{5,15},{6,12},{7,1},{8,14},{9,3},... | collective-permute-start | bytes 356360 | tf_op jit(solution)/shard_map/from_owners/ppermute | solution.py:331
  36.1 9.8 %collective-permute-start.9 = (f32[8,7,8,128]{3,2,1,0:T(8,128)S(1)}, f32[8,7,8,128]{3,2,1,0:T(8,128)S(1)}, u32[]{:S(2)}, u32[]{:S(2)}) collective-permute-start(f32[8,7,8,128]{3,2,1,0:T(8,128)S(1)} %get-tuple-element.71), channel_id=1, source_target_pairs={{0,1},{1,0},{2,3},{3,2},{4,5},{5,4},{6,7},{7,6},{8,9},{9,8},{10,11... | collective-permute-start | bytes 688136 | tf_op jit(solution)/shard_map/side_states/ppermute | solution.py:396
  37.8 8.3 %collective-permute-start.12 = (f32[58,8,128]{2,1,0:T(8,128)S(1)}, f32[58,8,128]{2,1,0:T(8,128)S(1)}, u32[]{:S(2)}, u32[]{:S(2)}) collective-permute-start(f32[58,8,128]{2,1,0:T(8,128)S(1)} %collect_first.1.first_ref.refs_0_), channel_id=1, source_target_pairs={{0,1},{1,0},{2,3},{3,2},{4,5},{5,4},{6,7},{7,6},{8,9},{9,8},{10,11... | collective-permute-start | bytes 712712 | tf_op jit(solution)/shard_map/first_states/ppermute | solution.py:402
  46.0 1.5 %collective-permute-start.13 = (f32[44,8,128]{2,1,0:T(8,128)S(1)}, f32[44,8,128]{2,1,0:T(8,128)S(1)}, u32[]{:S(2)}, u32[]{:S(2)}) collective-permute-start(f32[44,8,128]{2,1,0:T(8,128)S(1)} %collect_second.1.refs_1_), channel_id=1, source_target_pairs={{0,1},{1,0},{2,3},{3,2},{4,5},{5,4},{6,7},{7,6},{8,9},{9,8},{10,11... | collective-permute-start | bytes 540680 | tf_op jit(solution)/shard_map/states/ppermute | solution.py:422
  47.5 7.4 %collective-permute-start.16 = (f32[1,8,128]{2,1,0:T(8,128)S(1)}, f32[1,8,128]{2,1,0:T(8,128)S(1)}, u32[]{:S(2)}, u32[]{:S(2)}) collective-permute-start(f32[1,8,128]{2,1,0:T(8,128)S(1)} %slice_add_fusion), channel_id=1, source_target_pairs={{0,192},{64,0},{128,64},{192,128},{1,193},{65,1},{129,65},{193,129... | collective-permute-start | bytes 12296 | tf_op jit(solution)/shard_map/grad_gain/ppermute | solution.py:430
  50.3 5.1 %collective-permute-start.15 = (f32[1,8,128]{2,1,0:T(8,128)S(1)}, f32[1,8,128]{2,1,0:T(8,128)S(1)}, u32[]{:S(2)}, u32[]{:S(2)}) collective-permute-start(f32[1,8,128]{2,1,0:T(8,128)S(1)} %slice_add_fusion), channel_id=1, source_target_pairs={{0,128},{64,192},{128,0},{192,64},{1,129},{65,193},{129,1},{193,65... | collective-permute-start | bytes 12296 | tf_op jit(solution)/shard_map/grad_gain/ppermute | solution.py:430
  51.3 4.8 %collective-permute-start.14 = (f32[1,8,128]{2,1,0:T(8,128)S(1)}, f32[1,8,128]{2,1,0:T(8,128)S(1)}, u32[]{:S(2)}, u32[]{:S(2)}) collective-permute-start(f32[1,8,128]{2,1,0:T(8,128)S(1)} %slice_add_fusion), channel_id=1, source_target_pairs={{0,64},{64,128},{128,192},{192,0},{1,65},{65,129},{129,193},{193,1... | collective-permute-start | bytes 12296 | tf_op jit(solution)/shard_map/grad_gain/ppermute | solution.py:430
